TPU v7x, 128 devices: a whole 4x4x4 slice. The times are simulated.
128 devices in a mesh: tower: 2 (over x_lo), shard: 64 (over y, x_hi, z, core).
Axes of the slice: x: 4 (x_hi: 2, x_lo: 2; x = x_hi * 2 + x_lo), y: 4, z: 4, core: 2. Of those that a mesh axis runs over, the one named last changes fastest.
Arguments:
- tables: bfloat16 [2, 1048576, 256], P('tower', 'shard'), may hold values from -8 to 8
- bag_owner: int32 [2, 32768, 8], P('tower', 'shard'), may hold values from 0 to 63, all different within a row; in each aligned block of 512 rows (0 to 511, 512 to 1023, ..., all dimensions but the last counted through in order) at most 80 rows name the same one
- bag_block: int32 [2, 32768, 8], P('tower', 'shard'), may hold values from 0 to 127
- bag_offset: int32 [2, 32768, 8], P('tower', 'shard'), may hold values from 0 to 127
- bag_weight: float32 [2, 32768, 8], P('tower', 'shard'), may hold values from 0.2 to 1
- w_in: bfloat16 [2, 256, 2048], P('tower'), may hold values from -0.375 to 0.375
- w_out: bfloat16 [2, 2048, 256], P('tower'), may hold values from -0.125 to 0.125
- labels: int32 [32768], P('shard'), may hold values from 0 to 32767, each once
- logit_scale: float32 [], replicated, may hold values from 10 to 400
Outputs:
- losses: float32 [2, 32768], P('tower', 'shard')
Inputs may be any that keep to these rules, and one draw needn't show every extreme that they name: `bag_owner`: each row names 8 different owners. Among the rows of one device no owner is named more than 80 times, a bound that some block reaches. `labels`: every item index appears exactly once.
All inputs are finite; a program needn't handle non-finite values.
Results may differ from a plain program's by a relative error of at most 0.00072.
Values may be sent and summed in bfloat16 or wider, within the bound.
A program may use at most 192 MiB of HBM per device.

v0:
```python
import jax
import jax.numpy as jnp
from jax import lax
from jax.sharding import PartitionSpec as P

ROW_BLOCK = 128


def from_partner(block, axis, distance):
    count = lax.axis_size(axis)
    route = []
    for low in range(count):
        high = low | 1 << distance
        if high != low and high < count:
            route += [(low, high), (high, low)]
    return lax.ppermute(block, axis, route)


def update_rows(running, scores, positive_mask):
    top_now, sum_now, hit_now = running
    new_top = jnp.max(scores, axis=1)
    new_sum = sum_now * jnp.exp(top_now - new_top) + jnp.sum(
        jnp.exp(scores - new_top[:, None]), axis=1
    )
    new_hit = jnp.sum(jnp.where(positive_mask, scores, 0.0), axis=1)
    return (new_top, new_sum, new_hit)


def per_device(
    tables, bag_owner, bag_block, bag_offset, bag_weight, w_in, w_out, labels, logit_scale
):
    id_table = tables[0]
    width = id_table.shape[1]
    owner_ids = bag_owner[0].reshape(-1)
    local_row = (bag_block[0] * ROW_BLOCK + bag_offset[0]).reshape(-1)
    groups = lax.axis_size("shard")
    entries = owner_ids.shape[0]
    capacity = 8 * ((5 * entries + 32 * groups - 1) // (32 * groups))
    onehot = (owner_ids[:, None] == jnp.arange(groups, dtype=jnp.int32)[None, :]).astype(jnp.int32)
    slot_index = jnp.sum((jnp.cumsum(onehot, axis=0) - 1) * onehot, axis=1)
    target = owner_ids * capacity + slot_index
    requests = (
        jnp.zeros((groups * capacity,), jnp.int32)
        .at[target]
        .set(local_row)
        .reshape(groups, capacity)
    )
    asked_rows = lax.all_to_all(requests, "shard", split_axis=0, concat_axis=0, tiled=True)
    looked_up = jnp.take(id_table, asked_rows.reshape(-1), axis=0).reshape(
        asked_rows.shape[0], asked_rows.shape[1], width
    )
    fetched = lax.all_to_all(looked_up, "shard", split_axis=0, concat_axis=0, tiled=True)
    batch_rows = bag_weight.shape[1]
    gathered = jnp.take(fetched.reshape(groups * capacity, width), target, axis=0).reshape(
        batch_rows, bag_weight.shape[2], width
    )
    pooled = jnp.einsum("bk,bke->be", bag_weight[0], gathered.astype(jnp.float32)).astype(
        jnp.bfloat16
    )
    hidden = jax.nn.silu(jnp.dot(pooled, w_in[0], preferred_element_type=jnp.float32)).astype(
        jnp.bfloat16
    )
    widened = jnp.dot(hidden, w_out[0], preferred_element_type=jnp.float32) + pooled.astype(
        jnp.float32
    )
    embedding = (
        widened * lax.rsqrt(jnp.sum(widened * widened, axis=1, keepdims=True) + 1e-06)
    ).astype(jnp.bfloat16)
    partner = from_partner(embedding, "tower", 0)
    tower_index = lax.axis_index("tower")
    shard_index = lax.axis_index("shard")
    is_query = tower_index == 0
    row_index = shard_index * batch_rows + jnp.arange(batch_rows, dtype=jnp.int32)
    row_initial = (
        jnp.full((batch_rows,), -jnp.inf, jnp.float32),
        jnp.zeros((batch_rows,), jnp.float32),
        jnp.zeros((batch_rows,), jnp.float32),
    )
    key_rows = lax.all_gather(partner, "shard", axis=0, tiled=True)
    key_labels = lax.all_gather(labels, "shard", axis=0, tiled=True)
    count = key_rows.shape[0]
    col_index = jnp.arange(count, dtype=jnp.int32)
    positive_mask = jnp.where(
        is_query, labels[:, None] == col_index[None, :], key_labels[None, :] == row_index[:, None]
    )
    top_all, sum_all, hit_all = update_rows(
        row_initial,
        lax.dot_general(
            embedding, key_rows, (((1,), (1,)), ((), ())), preferred_element_type=jnp.float32
        )
        * logit_scale,
        positive_mask,
    )
    losses = top_all + jnp.log(sum_all) - hit_all
    return losses[None, :]


def solution(mesh):
    placed = (
        P("tower", "shard", None),
        P("tower", "shard", None),
        P("tower", "shard", None),
        P("tower", "shard", None),
        P("tower", "shard", None),
        P("tower", None, None),
        P("tower", None, None),
        P("shard"),
        P(),
    )
    return jax.shard_map(
        per_device, mesh=mesh, in_specs=placed, out_specs=P("tower", "shard"), check_vma=False
    )
```

profile of v0, /device:TPU:1, one launch (start us, length us, event | category | flops | bytes accessed | tf_op | source)
XLA Modules:
  0.0 356.8 jit_solution(4120298473004054934)
XLA Ops:
  6.5 0.9 copy.23
  7.8 0.7 broadcast_multiply_fusion
  8.6 18.4 %reduce-window.6 = s32[64,32,128]{2,1,0:T(8,128)S(1)} reduce-window(s32[64,32,128]{2,1,0:T(8,128)S(1)} %fusion.8, s32[]{:T(128)} %constant.22.clone.1), window={size=1x1x128 pad=0_0x0_0x127_0}, to_apply=%region_0.0 | reduce-window | flops 33292288 | bytes 2097156 | tf_op jit(solution)/shard_map/reduce-window
  27.4 0.4 copy.35
  29.0 0.8 fusion.4
  29.9 15.5 %scatter_custom_fusion = s32[5120]{0:T(1024)S(1)} fusion(s32[4096]{0:T(1024)S(1)} %bitcast.62, s32[4096]{0:T(1024)S(1)} %reshape.195, s32[]{:T(128)} %constant.22.clone.1), kind=kCustom, calls=%fused_computation.35 | custom fusion | bytes 20484 | tf_op jit(solution)/shard_map/scatter | solution.py:45
  45.6 21.6 %all_to_all.14 = s32[64,1,80]{2,1,0:T(1,128)S(1)} all-to-all(s32[64,1,80]{2,1,0:T(1,128)S(1)} %all_to_all.9), channel_id=1, replica_groups=mesh['tower'=2,'shard'=64] {'shard'}, dimensions={0} | all-to-all | bytes 40960 | tf_op jit(solution)/shard_map/all_to_all | solution.py:48
  67.1 0.5 broadcast.146
  67.6 0.7 reduce.5
  68.5 24.2 %gather_fusion = bf16[5120,256]{1,0:T(8,128)(2,1)} fusion(bf16[16384,256]{1,0:T(8,128)(2,1)} %bitcast.53, s32[5120]{0:T(1024)S(1)} %broadcast_clamp_fusion), kind=kCustom, calls=%fused_computation | custom fusion | bytes 5263360 | tf_op jit(solution)/shard_map/jit(_take)/gather | solution.py:49
  92.7 4.5 %broadcast_select_fusion = bf16[64,80,256]{2,1,0:T(8,128)(2,1)} fusion(bf16[64,80,256]{2,1,0:T(8,128)(2,1)} %bitcast.54, pred[64,80]{1,0:T(8,128)(4,1)S(1)} %compare_and_fusion), kind=kLoop, calls=%fused_computation.10 | loop fusion | flops 1310720 | bytes 5248000 | tf_op jit(solution)/shard_map/jit(_take)/select_n | solution.py:49
  97.2 5.7 %all-to-all-start.1 = ((bf16[64,80,256]{2,1,0:T(8,128)(2,1)}), bf16[64,80,256]{2,1,0:T(8,128)(2,1)}, u32[]{:S(2)}, u32[]{:S(2)}) async-start(bf16[64,80,256]{2,1,0:T(8,128)(2,1)} %broadcast_select_fusion), calls=%async_computation.1 | async-start | bytes 5242880 | tf_op jit(solution)/shard_map/all_to_all | solution.py:52
  103.5 35.4 %all-to-all-done.1 = bf16[64,80,256]{2,1,0:T(8,128)(2,1)} async-done(((bf16[64,80,256]{2,1,0:T(8,128)(2,1)}), bf16[64,80,256]{2,1,0:T(8,128)(2,1)}, u32[]{:S(2)}, u32[]{:S(2)}) %all-to-all-start.1) | async-done | bytes 2621472 | tf_op jit(solution)/shard_map/all_to_all | solution.py:52
  139.0 15.1 %gather_fusion.1 = bf16[4096,256]{1,0:T(8,128)(2,1)S(1)} fusion(bf16[5120,256]{1,0:T(8,128)(2,1)} %bitcast.10, s32[4096]{0:T(1024)S(1)} %broadcast_clamp_fusion.1), kind=kCustom, calls=%fused_computation.1 | custom fusion | bytes 4210688 | tf_op jit(solution)/shard_map/jit(_take)/gather | solution.py:54
  154.1 3.7 %multiply_reduce_fusion.1 = bf16[512,256]{1,0:T(8,128)(2,1)} fusion(f32[512,8]{1,0:T(8,128)S(1)} %copy.36, bf16[4096,256]{1,0:T(8,128)(2,1)S(1)} %gather_fusion.1, pred[512,8]{1,0:T(8,128)(4,1)S(1)} %copy.28), kind=kLoop, calls=%fused_computation.8 | loop fusion | flops 4063232 | bytes 2379776
  157.7 1.1 copy.34
  158.8 3.0 multiply_reduce_fusion.2
  162.4 7.5 %collective-permute-done = bf16[512,256]{0,1:T(8,128)(2,1)S(1)} collective-permute-done((bf16[512,256]{0,1:T(8,128)(2,1)S(1)}, bf16[512,256]{0,1:T(8,128)(2,1)S(1)}, u32[]{:S(2)}, u32[]{:S(2)}) %collective-permute-start) | collective-permute-done | bytes 262176 | tf_op jit(solution)/shard_map/ppermute | solution.py:16
  169.9 0.7 copy-done.1
  171.3 92.5 %all-gather = s32[64,1,512]{2,1,0:T(1,128)S(1)} all-gather(s32[1,1,512]{2,1,0:T(1,128)S(1)} %bitcast.66), channel_id=1, replica_groups=mesh['tower'=2,'shard'=64] {'shard'}, dimensions={0}, use_global_device_ids=true | all-gather | bytes 133120 | tf_op jit(solution)/shard_map/all_gather | solution.py:80
  263.8 21.2 %all-gather.3.cloned.1.call-done = bf16[32768,256]{0,1:T(8,128)(2,1)} async-done(((bf16[512,256]{0,1:T(8,128)(2,1)}), bf16[32768,256]{0,1:T(8,128)(2,1)}) %all-gather.3.cloned.1.call-update) | async-done | bytes 16777232 | tf_op jit(solution)/shard_map/all_gather | solution.py:79
  284.9 28.9 %multiply_reduce_fusion = (f32[512]{0:T(512)S(1)}, f32[512,32768]{1,0:T(8,128)}) fusion(f32[]{:T(128)S(6)} %copy.39, bf16[512,256]{0,1:T(8,128)(2,1)S(1)} %multiply_convert_fusion.1, bf16[32768,256]{0,1:T(8,128)(2,1)} %all-gather.3.cloned.1.call-done), kind=kOutput, calls=%fused_computation.7 | convolution fusion | flops 8623489024 | bytes 84150272 | tf_op jit(solution)/shard_map/dot_general | solution.py:88
  313.9 35.5 %exponential_reduce_fusion = (f32[512]{0:T(512)S(1)}, f32[512]{0:T(512)S(1)}) fusion(f32[512,32768]{1,0:T(8,128)} %get-tuple-element.10, f32[512]{0:T(512)S(1)} %get-tuple-element.9, f32[]{:T(128)S(6)} %copy.39, s32[512]{0:T(512)S(1)} %iota_add_fusion, s32[32768]{0:T(1024)S(1)} %bitcast.56, s32[512]{0:T(512)S(1)} %copy-done.6, pred[]{:T(512)S(6)} %eq.59), kind=kLoop, calls=%fused_computation.5 | loop fusion | flops 134216704 | bytes 67250184 | tf_op jit(solution)/shard_map/reduce_sum | solution.py:22
  349.3 0.6 add_subtract_fusion
  (42 shorter events, 3.3 us)
Async XLA Ops:
  6.5 152.3 %copy-start = (bf16[1,2048,256]{2,1,0:T(8,128)(2,1)S(1)}, bf16[1,2048,256]{2,1,0:T(8,128)(2,1)}, u32[]{:S(2)}) copy-start(bf16[1,2048,256]{2,1,0:T(8,128)(2,1)} %param.15) | copy-start | bytes 3145732
  8.6 20.1 %copy-start.3 = (s32[1,512,8]{1,2,0:T(8,128)S(1)}, s32[1,512,8]{1,2,0:T(8,128)}, u32[]{:S(2)}) copy-start(s32[1,512,8]{1,2,0:T(8,128)} %param.12) | copy-start | bytes 49156
  8.6 20.1 %copy-start.4 = (s32[1,512,8]{1,2,0:T(8,128)S(1)}, s32[1,512,8]{1,2,0:T(8,128)}, u32[]{:S(2)}) copy-start(s32[1,512,8]{1,2,0:T(8,128)} %param.11) | copy-start | bytes 49156
  97.2 6.0 %copy-start.2 = (s32[1,512,8]{1,2,0:T(8,128)S(1)}, s32[1,512,8]{1,2,0:T(8,128)}, u32[]{:S(2)}) copy-start(s32[1,512,8]{1,2,0:T(8,128)} %param.10) | copy-start | bytes 49156
  97.2 6.2 %copy-start.5 = (f32[1,512,8]{1,2,0:T(8,128)S(1)}, f32[1,512,8]{1,2,0:T(8,128)}, u32[]{:S(2)}) copy-start(f32[1,512,8]{1,2,0:T(8,128)} %param.13) | copy-start | bytes 49156
  97.2 41.8 %all-to-all-start.1 = ((bf16[64,80,256]{2,1,0:T(8,128)(2,1)}), bf16[64,80,256]{2,1,0:T(8,128)(2,1)}, u32[]{:S(2)}, u32[]{:S(2)}) async-start(bf16[64,80,256]{2,1,0:T(8,128)(2,1)} %broadcast_select_fusion), calls=%async_computation.1 | async-start | bytes 5242880 | tf_op jit(solution)/shard_map/all_to_all | solution.py:52
  102.9 182.0 %all-gather.3.cloned.1.call-start = ((), (), s32[]{:S(2)}) async-start(), calls=%async_computation.2 | async-start | bytes 17039360 | tf_op jit(solution)/shard_map/all_gather | solution.py:79
  158.8 12.4 %copy-start.6 = (s32[512]{0:T(512)S(1)}, s32[512]{0:T(512)}, u32[]{:S(2)}) copy-start(s32[512]{0:T(512)} %param.16) | copy-start | bytes 6148
  161.9 8.0 %collective-permute-start = (bf16[512,256]{0,1:T(8,128)(2,1)S(1)}, bf16[512,256]{0,1:T(8,128)(2,1)S(1)}, u32[]{:S(2)}, u32[]{:S(2)}) collective-permute-start(bf16[512,256]{0,1:T(8,128)(2,1)S(1)} %multiply_convert_fusion.1), channel_id=1, source_target_pairs={{0,64},{64,0},{1,65},{65,1},{2,66},{66,2},{3,67},{67,3},{4,68},{68... | collective-permute-start | bytes 786440 | tf_op jit(solution)/shard_map/ppermute | solution.py:16
  169.9 0.7 copy-start.1
Sparse Core Ops, SparseCore 0:
  170.7 114.1 all-gather.2
where the time goes:
time: 357 us
  blocking collectives  114 us (32%)
  other arithmetic  65.7 us (18%)
  waiting for transfers between devices  64.1 us (18%)
  local copies, waits for them, and re-layouts  60.4 us (17%)
  matrix products  32 us (9%)
  between operations  14.3 us (4%)
  starting transfers between devices  6.19 us (2%)
    all_gather x1, blocking collectives, per_device(): key_labels = lax.all_gather(labels, 'shard', axis=0, tiled=True)  92.5 us
    reduce_sum x1, other arithmetic, update_rows(): jnp.sum(jnp.exp(scores - new_top[:, None]), axis=1)  35.5 us
    all_to_all x1, waiting for transfers between devices, per_device(): lax.all_to_all(looked_up, 'shard', split_axis=0, concat_axis=0, tiled=True)  35.4 us
    dot_general x1, matrix products, per_device(): lax.dot_general(embedding, key_rows, (((1,), (1,)), ((), ())), preferred_...  28.9 us
    gather x1, local copies, waits for them, and re-layouts, per_device(): jnp.take(id_table, asked_rows.reshape(-1), axis=0)  24.2 us
    all_to_all x1, blocking collectives, per_device(): lax.all_to_all(requests, 'shard', split_axis=0, concat_axis=0, tiled=True)  21.6 us
    all_gather x1, waiting for transfers between devices, per_device(): key_rows = lax.all_gather(partner, 'shard', axis=0, tiled=True)  21.2 us
    another operation x2, other arithmetic  18.6 us
  transfers between devices with their start and end apart: 3, of which 3 were waited for; matrix products, arithmetic and copies ran while one was open for 0% of the time, Pallas kernels for 0%

commit v1 on v0

v1 whole, which is shorter than its diff:
```python
import functools

import jax
import jax.numpy as jnp
from jax import lax
from jax.experimental import pallas as pl
from jax.experimental.pallas import tpu as pltpu
from jax.sharding import PartitionSpec as P

ROW_BLOCK = 128
RING = 4
CORES = 2
LOG2E = 1.4426950408889634
LN2 = 0.6931471805599453
LOWEST = -1e30
MESH = pl.DeviceIdType.MESH


def whereabouts():
    tower = lax.axis_index("tower")
    shard = lax.axis_index("shard")
    return tower, shard // 16, shard // 8 % 2, shard // 2 % 4, shard % 2


def shard_at(y, x_hi, z, core):
    return ((y * 2 + x_hi) * 4 + z) * 2 + core


def own_line(position, core=None):
    tower, y, x_hi, z, c = whereabouts()
    c = c if core is None else core
    return shard_at(y + tower * (position - y), x_hi, z + (1 - tower) * (position - z), c)


def cross_line(position, core=None):
    tower, y, x_hi, z, c = whereabouts()
    c = c if core is None else core
    return shard_at(y + (1 - tower) * (position - y), x_hi, z + tower * (position - z), c)


def below_line(position, core):
    tower, y, x_hi, z, _ = whereabouts()
    plane = x_hi * tower + (1 - x_hi) * (1 - tower)
    return shard_at(y + tower * (position - y), plane, z + (1 - tower) * (position - z), core)


def above_line(position, core):
    tower, y, x_hi, z, _ = whereabouts()
    plane = x_hi * (1 - tower) + (1 - x_hi) * tower
    return shard_at(y + (1 - tower) * (position - y), plane, z + tower * (position - z), core)


def fold_lanes(op, x):
    parts = [x[:, q : q + 128] for q in range(0, x.shape[1], 128)]
    return functools.reduce(op, parts)


def fold_rows(op, x):
    parts = [x[r : r + 8] for r in range(0, x.shape[0], 8)]
    while len(parts) > 1:
        parts = [op(a, b) for a, b in zip(parts[::2], parts[1::2])]
    return parts[0]


def loss_kernel(
    emb_ref, labels_ref, scale_ref, out_ref,
    own, other, own_labels, other_labels, scores, row_key, row_max, row_sum, row_hit, col_max, col_sum, col_hit,
    row_note, col_note, row_post, col_post,
    own_send, own_recv, down_send, cross_send, swap_send, other_recv,
    row_send, row_recv, col_send, col_recv,
    own_label_send, own_label_recv, other_label_send, other_label_recv,
):
    rows = emb_ref.shape[0]
    tower, y, x_hi, z, core = whereabouts()
    mine = z + tower * (y - z)
    cross = y + tower * (z - y)
    scale = scale_ref[0, 0]
    to_log2 = scale * LOG2E

    barrier = pltpu.get_barrier_semaphore()

    def greet(tower_id, shard_id):
        pl.semaphore_signal(barrier, inc=1, device_id=(tower_id, shard_id), device_id_type=MESH)

    for step in range(1, RING):
        greet(tower, own_line((mine + step) % RING))
        greet(tower, cross_line((cross + step) % RING))
    greet(tower, own_line(mine, 1 - core))
    for p in range(RING):
        for c in range(CORES):
            greet(1 - tower, below_line(p, c))
            greet(1 - tower, above_line(p, c))
    pl.semaphore_wait(barrier, 2 * (RING - 1) + 1 + 2 * RING * CORES)

    def push(src, dst, send, recv, tower_id, shard_id):
        copy = pltpu.make_async_remote_copy(
            src_ref=src, dst_ref=dst, send_sem=send, recv_sem=recv,
            device_id=(tower_id, shard_id), device_id_type=MESH,
        )
        copy.start()
        return copy

    def arrived(ref, sem):
        pltpu.make_async_copy(ref, ref, sem).wait()

    sent = []
    sent.append(push(emb_ref, other.at[core, mine], down_send.at[0], other_recv.at[core, mine],
                     1 - tower, below_line(mine, core)))
    for step in (1, 3, 2):
        sent.append(push(emb_ref, own.at[mine], own_send.at[step], own_recv.at[mine],
                         tower, own_line((mine + step) % RING)))
    for step in (1, 3, 2):
        sent.append(push(labels_ref, own_labels.at[mine], own_label_send.at[step],
                         own_label_recv.at[mine], tower, own_line((mine + step) % RING)))
    for p in range(RING):
        for c in range(CORES):
            sent.append(push(labels_ref, other_labels.at[core, mine], other_label_send.at[c, p],
                             other_label_recv.at[core, mine], 1 - tower, below_line(p, c)))
    own[mine] = emb_ref[...]
    own_labels[mine] = labels_ref[...]

    for step in (1, 3, 2):
        position = (mine + step) % RING
        arrived(own_labels.at[position], own_label_recv.at[position])
    for p in range(RING):
        for c in range(CORES):
            arrived(other_labels.at[c, p], other_label_recv.at[c, p])
    for p in range(RING):
        ids = own_line(p) * rows + lax.broadcasted_iota(jnp.int32, (1, rows), 1)
        key = jnp.where(tower == 0, own_labels[p], ids)
        row_key[p] = jnp.transpose(jnp.broadcast_to(key, (128, rows)))

    def pass_on(position, which):
        here = other.at[core, position]
        return push(here, here, swap_send.at[which], other_recv.at[core, position],
                    tower, own_line(mine, 1 - core))

    here = other.at[core, cross]
    arrived(here, other_recv.at[core, cross])
    for step in (1, 3, 2):
        sent.append(push(here, here, cross_send.at[step], other_recv.at[core, cross],
                         tower, cross_line((cross + step) % RING)))
    sent.append(pass_on(cross, 0))
    for step in (1, 3, 2):
        position = (cross + step) % RING
        arrived(other.at[core, position], other_recv.at[core, position])
        sent.append(pass_on(position, step))
    for step in (1, 3, 2):
        position = (mine + step) % RING
        arrived(own.at[position], own_recv.at[position])

    width = RING * rows
    for half in range(CORES):
        side = (core + half) % CORES
        if half == 1:
            for p in range(RING):
                arrived(other.at[side, p], other_recv.at[side, p])
        col_max[half] = jnp.full((8, width), LOWEST, jnp.float32)
        col_sum[half] = jnp.zeros((8, width), jnp.float32)
        col_hit[half] = jnp.zeros((8, width), jnp.float32)

        for b in range(RING):
            cols = slice(b * rows, (b + 1) * rows)

            def product(a, carry, b=b, cols=cols):
                s = lax.dot_general(own[a], other[side, b], (((1,), (1,)), ((), ())),
                                    preferred_element_type=jnp.float32)
                scores[a, :, cols] = s
                top = fold_lanes(jnp.maximum, s)
                row_max[half, a] = top if b == 0 else jnp.maximum(row_max[half, a], top)
                return jnp.maximum(carry, fold_rows(jnp.maximum, s))

            col_max[half, :, cols] = lax.fori_loop(
                0, RING, product, jnp.full((8, rows), LOWEST, jnp.float32))

        strip = 32
        for b in range(RING):
            cols = slice(b * rows, (b + 1) * rows)
            shard = above_line(b, side)
            ids = shard * rows + lax.broadcasted_iota(jnp.int32, (1, rows), 1)
            col_key = jnp.where(tower == 0, ids, other_labels[side, b])
            col_top = col_max[half, :, cols] * to_log2
            col_top_strip = jnp.concatenate([col_top] * (strip // 8), axis=0)
            col_key_strip = jnp.broadcast_to(col_key, (strip, rows))

            def sums(i, carry, b=b, cols=cols, col_top_strip=col_top_strip, col_key_strip=col_key_strip):
                c_sum, c_hit = carry
                a = i // (rows // strip)
                at = pl.ds(pl.multiple_of(i % (rows // strip) * strip, strip), strip)
                s = scores[a, at, cols]
                t = s * to_log2
                top = row_max[half, a, at] * to_log2
                key = row_key[a, at]
                lanes = [slice(q, q + 128) for q in range(0, rows, 128)]
                r_sum = sum(jnp.exp2(t[:, q] - top) for q in lanes)
                hits = [jnp.where(key == col_key_strip[:, q], s[:, q], 0.0) for q in lanes]
                r_hit = sum(hits)
                if b == 0:
                    row_sum[half, a, at] = r_sum
                    row_hit[half, a, at] = r_hit
                else:
                    row_sum[half, a, at] += r_sum
                    row_hit[half, a, at] += r_hit
                c_sum = c_sum + fold_rows(jnp.add, jnp.exp2(t - col_top_strip))
                c_hit = c_hit + fold_rows(jnp.add, jnp.concatenate(hits, axis=1))
                return c_sum, c_hit

            zero = jnp.zeros((8, rows), jnp.float32)
            c_sum, c_hit = lax.fori_loop(0, RING * rows // strip, sums, (zero, zero))
            top = jnp.max(col_top, axis=0, keepdims=True)
            total = jnp.sum(c_sum * jnp.exp2(col_top - top), axis=0, keepdims=True)
            hit = jnp.sum(c_hit, axis=0, keepdims=True)
            col_note[half, b] = jnp.concatenate(
                [top, total, hit, jnp.zeros((5, rows), jnp.float32)], axis=0)
            sent.append(push(col_note.at[half, b], col_post.at[cross, core], col_send.at[half, b],
                             col_recv.at[cross, core], 1 - tower, above_line(b, side)))

    lane = lax.broadcasted_iota(jnp.int32, (rows, 128), 1)

    def row_totals(a, carry):
        tops = [row_max[half, a] * to_log2 for half in range(CORES)]
        top = jnp.max(jnp.maximum(*tops), axis=1, keepdims=True)
        total = jnp.sum(sum(row_sum[half, a] * jnp.exp2(tops[half] - top) for half in range(CORES)),
                        axis=1, keepdims=True)
        hit = jnp.sum(row_hit[0, a] + row_hit[1, a], axis=1, keepdims=True)
        packed = jnp.where(lane == 0, top, jnp.where(lane == 1, total, jnp.where(lane == 2, hit, 0.0)))
        row_note[a] = jnp.transpose(packed)[:8]
        return carry

    lax.fori_loop(0, RING, row_totals, 0)
    for step in (1, 2, 3):
        position = (mine + step) % RING
        sent.append(push(row_note.at[position], row_post.at[mine], row_send.at[step],
                         row_recv.at[mine], tower, own_line(position)))
    for step in (1, 2, 3):
        position = (mine + step) % RING
        arrived(row_post.at[position], row_recv.at[position])
    for p in range(RING):
        for c in range(CORES):
            arrived(col_post.at[p, c], col_recv.at[p, c])
    row_post[mine] = row_note[mine]
    notes = [row_post[p] for p in range(RING)]
    notes += [col_post[p, c] for p in range(RING) for c in range(CORES)]
    top = functools.reduce(jnp.maximum, [n[0:1] for n in notes])
    total = sum(n[1:2] * jnp.exp2(n[0:1] - top) for n in notes)
    hit = sum(n[2:3] for n in notes)
    out_ref[...] = LN2 * top + jnp.log(total) - scale * hit
    for copy in sent:
        copy.wait_send()


def in_batch_losses(embedding, labels, logit_scale):
    rows, width = embedding.shape
    f32 = jnp.float32
    dma = pltpu.SemaphoreType.DMA
    wide = RING * rows
    return pl.pallas_call(
        loss_kernel,
        out_shape=jax.ShapeDtypeStruct((1, rows), f32),
        in_specs=[
            pl.BlockSpec(memory_space=pltpu.VMEM),
            pl.BlockSpec(memory_space=pltpu.VMEM),
            pl.BlockSpec(memory_space=pltpu.SMEM),
        ],
        out_specs=pl.BlockSpec(memory_space=pltpu.VMEM),
        scratch_shapes=[
            pltpu.VMEM((RING, rows, width), jnp.bfloat16),
            pltpu.VMEM((CORES, RING, rows, width), jnp.bfloat16),
            pltpu.VMEM((RING, 1, rows), jnp.int32),
            pltpu.VMEM((CORES, RING, 1, rows), jnp.int32),
            pltpu.VMEM((RING, rows, wide), f32),
            pltpu.VMEM((RING, rows, 128), jnp.int32),
            pltpu.VMEM((CORES, RING, rows, 128), f32),
            pltpu.VMEM((CORES, RING, rows, 128), f32),
            pltpu.VMEM((CORES, RING, rows, 128), f32),
            pltpu.VMEM((CORES, 8, wide), f32),
            pltpu.VMEM((CORES, 8, wide), f32),
            pltpu.VMEM((CORES, 8, wide), f32),
            pltpu.VMEM((RING, 8, rows), f32),
            pltpu.VMEM((CORES, RING, 8, rows), f32),
            pltpu.VMEM((RING, 8, rows), f32),
            pltpu.VMEM((RING, CORES, 8, rows), f32),
            dma((RING,)), dma((RING,)), dma((1,)), dma((RING,)), dma((RING,)), dma((CORES, RING)),
            dma((RING,)), dma((RING,)), dma((CORES, RING)), dma((RING, CORES)),
            dma((RING,)), dma((RING,)), dma((CORES, RING)), dma((CORES, RING)),
        ],
        compiler_params=pltpu.CompilerParams(
            collective_id=1, has_side_effects=True, vmem_limit_bytes=56 * 1024 * 1024
        ),
        cost_estimate=pl.CostEstimate(
            flops=2 * wide * 2 * wide * width, bytes_accessed=2 * rows * width, transcendentals=4 * wide * wide
        ),
        name="in_batch_losses",
    )(embedding, labels.reshape(1, rows), logit_scale.reshape(1, 1))


TABLE_PARTS = 8
SOURCES_AT_ONCE = 16


def pool_kernel(
    owner_ref, block_ref, offset_ref, weight_ref, w_in_ref, w_out_ref, table_ref, out_ref,
    table_16, table_32, ask, asked, asked_at, staged, outgoing, fetched, target_wide, weight_wide,
    mix_high, mix_low, pooled_sum, pooled_16,
    table_sem, ask_send, ask_recv, asked_sem, rows_send, rows_recv,
):
    f32, bf16 = jnp.float32, jnp.bfloat16
    bag, rows = owner_ref.shape
    groups, _, lanes = ask.shape
    capacity = outgoing.shape[0] // groups
    tower, y, x_hi, z, core = whereabouts()
    me = lax.axis_index("shard")

    def partner(i):
        offset = i * 27 % groups
        return shard_at((y + offset // 16) % 4, (x_hi + offset // 8) % 2, (z + offset // 2) % 4,
                        (core + offset) % 2)

    def block_of(ref, p):
        return ref.at[pl.ds(pl.multiple_of(p * capacity, 16), capacity)]

    part = table_16.shape[0] // TABLE_PARTS
    loads = []
    for i in range(TABLE_PARTS):
        at = pl.ds(i * part, part)
        loads.append(pltpu.make_async_copy(table_ref.at[at], table_16.at[at], table_sem.at[i]))
        loads[-1].start()

    barrier = pltpu.get_barrier_semaphore()

    def greet(i, carry):
        pl.semaphore_signal(barrier, inc=1, device_id=(tower, partner(i)), device_id_type=MESH)
        return carry

    lax.fori_loop(1, groups, greet, 0)

    group = lax.broadcasted_iota(jnp.int32, (groups, rows), 0)
    owners = [owner_ref[k : k + 1, :] for k in range(bag)]
    named = [owners[k] == group for k in range(bag)]
    count = sum(jnp.where(n, 1.0, 0.0) for n in named)
    before = jnp.where(
        lax.broadcasted_iota(jnp.int32, (rows, rows), 0) < lax.broadcasted_iota(jnp.int32, (rows, rows), 1),
        1.0, 0.0).astype(bf16)
    place = jnp.dot(count.astype(bf16), before, preferred_element_type=f32)
    lane_of = lax.broadcasted_iota(jnp.int32, (lanes, rows), 0).astype(f32)
    wanted = jnp.zeros((2 * groups, lanes), f32)
    for k in range(bag):
        slot = jnp.sum(jnp.where(named[k], place, 0.0), axis=0, keepdims=True)
        block = jnp.where(named[k], block_ref[k : k + 1, :].astype(f32), 0.0)
        offset = jnp.where(named[k], offset_ref[k : k + 1, :].astype(f32), 0.0)
        taken = jnp.where(lane_of == slot, 1.0, 0.0).astype(bf16)
        wanted += lax.dot_general(jnp.concatenate([block, offset], axis=0).astype(bf16), taken,
                                  (((1,), (1,)), ((), ())), preferred_element_type=f32)
        target_wide[k] = jnp.transpose(
            jnp.broadcast_to(owners[k].astype(f32) * capacity + slot, (lanes, rows)))
        weight_wide[k] = jnp.transpose(jnp.broadcast_to(weight_ref[k : k + 1, :], (lanes, rows)))
    wanted = (wanted[:groups] * ROW_BLOCK + wanted[groups:]).astype(jnp.int32)
    wanted = jnp.clip(wanted, 0, table_32.shape[0] - 1)
    for g in range(groups):
        ask[g] = wanted[g : g + 1]

    pl.semaphore_wait(barrier, groups - 1)

    def request(i, p):
        return pltpu.make_async_remote_copy(
            src_ref=ask.at[p], dst_ref=asked.at[me], send_sem=ask_send.at[p], recv_sem=ask_recv.at[me],
            device_id=(tower, p), device_id_type=MESH)

    def send_request(i, carry):
        request(i, partner(i)).start()
        return carry

    lax.fori_loop(1, groups, send_request, 0)
    asked[me] = ask[me]

    for i in range(TABLE_PARTS):
        loads[i].wait()

        def widen(j, carry, i=i):
            at = pl.ds(pl.multiple_of(i * part + j * 64, 64), 64)
            table_32[at] = table_16[at].astype(f32)
            return carry

        lax.fori_loop(0, part // 64, widen, 0)

    def request_arrived(i, carry):
        p = partner(i)
        pltpu.make_async_copy(asked.at[p], asked.at[p], ask_recv.at[p]).wait()
        return carry

    lax.fori_loop(1, groups, request_arrived, 0)
    to_scalar = pltpu.make_async_copy(asked, asked_at, asked_sem)
    to_scalar.start()
    to_scalar.wait()

    def look_up(p, destination):
        for c in range(capacity):
            row = jnp.clip(asked_at[p, 0, c], 0, table_32.shape[0] - 1)
            staged[c : c + 1] = table_32[pl.ds(row, 1)]
        destination[...] = staged[...].astype(bf16)

    def send_rows(p):
        return pltpu.make_async_remote_copy(
            src_ref=block_of(outgoing, p), dst_ref=block_of(fetched, me), send_sem=rows_send.at[p],
            recv_sem=rows_recv.at[me], device_id=(tower, p), device_id_type=MESH)

    def serve(i, carry):
        p = partner(i)
        look_up(p, block_of(outgoing, p))
        send_rows(p).start()
        return carry

    lax.fori_loop(1, groups, serve, 0)
    look_up(me, block_of(fetched, me))

    lane = lax.broadcasted_iota(jnp.int32, (16, lanes), 1).astype(f32)
    spread = mix_high.shape[1] // lanes

    def weigh(i, carry):
        at = pl.ds(pl.multiple_of(i * 16, 16), 16)
        targets = [target_wide[k, at] for k in range(bag)]
        weights = [weight_wide[k, at] for k in range(bag)]

        def column(j, carry):
            here = lane + (j * lanes).astype(f32)
            mixed = jnp.zeros((16, lanes), f32)
            for k in range(bag):
                mixed = jnp.where(targets[k] == here, weights[k], mixed)
            high = mixed.astype(bf16)
            cols = pl.ds(pl.multiple_of(j * lanes, lanes), lanes)
            mix_high[at, cols] = high
            mix_low[at, cols] = (mixed - high.astype(f32)).astype(bf16)
            return carry

        return lax.fori_loop(0, spread, column, carry, unroll=4)

    lax.fori_loop(0, rows // 16, weigh, 0)

    def rows_arrived(i, carry):
        p = partner(i)
        here = block_of(fetched, p)
        pltpu.make_async_copy(here, here, rows_recv.at[p]).wait()
        return carry

    lax.fori_loop(1, groups, rows_arrived, 0)

    deep = SOURCES_AT_ONCE * capacity
    pooled_sum[...] = jnp.zeros(pooled_sum.shape, f32)

    def pool(i, carry):
        at = pl.ds(pl.multiple_of(i * deep, deep), deep)
        data = fetched[at]
        pooled_sum[...] += (
            jnp.dot(mix_high[:, at], data, preferred_element_type=f32)
            + jnp.dot(mix_low[:, at], data, preferred_element_type=f32))
        return carry

    lax.fori_loop(0, groups // SOURCES_AT_ONCE, pool, 0)
    pooled_16[...] = pooled_sum[...].astype(bf16)
    pooled_sum[...] = pooled_16[...].astype(f32)
    hidden_part = 256

    def layer(i, carry):
        at = pl.ds(pl.multiple_of(i * hidden_part, hidden_part), hidden_part)
        v = jnp.dot(pooled_16[...], w_in_ref[:, at], preferred_element_type=f32)
        hidden = (v / (1.0 + jnp.exp(-v))).astype(bf16)
        pooled_sum[...] += jnp.dot(hidden, w_out_ref[at, :], preferred_element_type=f32)
        return carry

    lax.fori_loop(0, w_in_ref.shape[1] // hidden_part, layer, 0)
    widened = pooled_sum[...]
    out_ref[...] = (widened * lax.rsqrt(jnp.sum(widened * widened, axis=1, keepdims=True) + 1e-06)).astype(bf16)

    def finish(i, carry):
        p = partner(i)
        request(i, p).wait_send()
        send_rows(p).wait_send()
        return carry

    lax.fori_loop(1, groups, finish, 0)


def tower_embeddings(table, owner, block, offset, weight, w_in, w_out):
    bag, rows = owner.shape
    groups = lax.axis_size("shard")
    capacity = 8 * ((5 * bag * rows + 32 * groups - 1) // (32 * groups))
    width = table.shape[1]
    lanes = 128
    f32, bf16 = jnp.float32, jnp.bfloat16
    dma = pltpu.SemaphoreType.DMA
    slots = groups * capacity
    vmem = pl.BlockSpec(memory_space=pltpu.VMEM)
    return pl.pallas_call(
        pool_kernel,
        out_shape=jax.ShapeDtypeStruct((rows, width), bf16),
        in_specs=[vmem] * 6 + [pl.BlockSpec(memory_space=pl.ANY)],
        out_specs=vmem,
        scratch_shapes=[
            pltpu.VMEM(table.shape, bf16),
            pltpu.VMEM(table.shape, f32),
            pltpu.VMEM((groups, 1, lanes), jnp.int32),
            pltpu.VMEM((groups, 1, lanes), jnp.int32),
            pltpu.SMEM((groups, 1, lanes), jnp.int32),
            pltpu.VMEM((capacity, width), f32),
            pltpu.VMEM((slots, width), bf16),
            pltpu.VMEM((slots, width), bf16),
            pltpu.VMEM((bag, rows, lanes), f32),
            pltpu.VMEM((bag, rows, lanes), f32),
            pltpu.VMEM((rows, slots), bf16),
            pltpu.VMEM((rows, slots), bf16),
            pltpu.VMEM((rows, width), f32),
            pltpu.VMEM((rows, width), bf16),
            dma((TABLE_PARTS,)), dma((groups,)), dma((groups,)), dma, dma((groups,)), dma((groups,)),
        ],
        compiler_params=pltpu.CompilerParams(
            collective_id=2, has_side_effects=True, vmem_limit_bytes=58 * 1024 * 1024
        ),
        cost_estimate=pl.CostEstimate(
            flops=4 * rows * slots * width, bytes_accessed=2 * table.size, transcendentals=rows * w_in.shape[1]
        ),
        name="tower_embeddings",
    )(owner, block, offset, weight, w_in, w_out, table)


def per_device(
    tables, bag_owner, bag_block, bag_offset, bag_weight, w_in, w_out, labels, logit_scale
):
    embedding = tower_embeddings(
        tables[0], bag_owner[0].T, bag_block[0].T, bag_offset[0].T, bag_weight[0].T, w_in[0], w_out[0]
    )
    return in_batch_losses(embedding, labels, logit_scale)


def solution(mesh):
    placed = (
        P("tower", "shard", None),
        P("tower", "shard", None),
        P("tower", "shard", None),
        P("tower", "shard", None),
        P("tower", "shard", None),
        P("tower", None, None),
        P("tower", None, None),
        P("shard"),
        P(),
    )
    return jax.shard_map(
        per_device, mesh=mesh, in_specs=placed, out_specs=P("tower", "shard"), check_vma=False
    )
```

time: 357 us -> 137 us (0.38)
  Pallas kernels: 0 us -> 134 us
  blocking collectives: 114 us -> 0 us
  other arithmetic: 65.7 us -> 0 us
  waiting for transfers between devices: 64.1 us -> 0 us
  local copies, waits for them, and re-layouts: 60.4 us -> 1.24 us
  matrix products: 32 us -> 0 us
  between operations: 14.3 us -> 0.67 us
  starting transfers between devices: 6.19 us -> 0 us
    pallas_call x0 -> x2, Pallas kernels: none -> 134 us  [the longest x1 67.3 us: tower_embeddings(): pl.pallas_call(pool_kernel, out_shape=jax.ShapeDtypeStruct((rows, width),...]
    all_gather x1 -> x0, blocking collectives: 92.5 us -> none  [per_device(): key_labels = lax.all_gather(labels, 'shard', axis=0, tiled=True)]
    gather x2 -> x0, local copies, waits for them, and re-layouts: 39.2 us -> none  [the longest x1 24.2 us: per_device(): jnp.take(id_table, asked_rows.reshape(-1), axis=0)]
    reduce_sum x2 -> x0, other arithmetic: 36.3 us -> none  [the longest x1 35.5 us: update_rows(): jnp.sum(jnp.exp(scores - new_top[:, None]), axis=1)]
    all_to_all x1 -> x0, waiting for transfers between devices: 35.4 us -> none  [per_device(): lax.all_to_all(looked_up, 'shard', split_axis=0, concat_axis=0, tiled=True)]
    dot_general x2 -> x0, matrix products: 32 us -> none  [the longest x1 28.9 us: per_device(): lax.dot_general(embedding, key_rows, (((1,), (1,)), ((), ())), preferred_...]
    all_to_all x1 -> x0, blocking collectives: 21.6 us -> none  [per_device(): lax.all_to_all(requests, 'shard', split_axis=0, concat_axis=0, tiled=True)]
    all_gather x1 -> x0, waiting for transfers between devices: 21.2 us -> none  [per_device(): key_rows = lax.all_gather(partner, 'shard', axis=0, tiled=True)]
  transfers between devices with their start and end apart: 3 -> 0, of which waited for: 3 -> 0; matrix products, arithmetic and copies ran while one was open for 0% -> 0% of each run, Pallas kernels for 0% -> 0%
where the time goes in v1:
time: 137 us; the launch traced here: 136 us
  Pallas kernels  134 us (98%)
    pallas_call x1, Pallas kernels, tower_embeddings(): pl.pallas_call(pool_kernel, out_shape=jax.ShapeDtypeStruct((rows, width),...  67.3 us
    pallas_call x1, Pallas kernels, in_batch_losses(): pl.pallas_call(loss_kernel, out_shape=jax.ShapeDtypeStruct((1, rows), f32...  66.9 us

profile of v1, /device:TPU:1, one launch (start us, length us, event | category | flops | bytes accessed | tf_op | source)
XLA Modules:
  0.0 136.2 jit_solution(17089120742750228429)
XLA Ops:
  0.7 67.3 %tower_embeddings.1.emb_ref = bf16[512,256]{1,0:T(8,128)(2,1)} custom-call(s32[8,512]{1,0:T(8,128)} %bitcast.21, s32[8,512]{1,0:T(8,128)} %bitcast.22, s32[8,512]{1,0:T(8,128)} %bitcast.23, f32[8,512]{1,0:T(8,128)} %bitcast.24, bf16[256,2048]{1,0:T(8,128)(2,1)} %bitcast.19, bf16[2048,256]{1,0:T(8,128)(2,1)} %bitcast.20, bf16[16384,256]{1,0:T(8,128)(2,1)} %bitcast.18), custom_call_target="tpu_custom_call" | custom-call | flops 2684354560 | bytes 8388608 | tf_op jit(solution)/shard_map/tower_embeddings/pallas_call | solution.py:493
  68.0 66.9 %in_batch_losses.1 = f32[1,512]{1,0:T(1,128)} custom-call(bf16[512,256]{1,0:T(8,128)(2,1)} %tower_embeddings.1.emb_ref, s32[1,512]{1,0:T(1,128)} %bitcast.25, f32[1,1]{1,0:T(1,128)} %bitcast.17.scale_ref), custom_call_target="tpu_custom_call" | custom-call | flops 4294967296 | bytes 262144 | tf_op jit(solution)/shard_map/in_batch_losses/pallas_call | solution.py:257
  134.9 1.2 copy.12

commit v2 on v0

v2 whole, which is shorter than its diff:
```python
import jax
import jax.numpy as jnp
from jax import lax
from jax.experimental import pallas as pl
from jax.experimental.pallas import tpu as pltpu
from jax.sharding import PartitionSpec as P

ROW_BLOCK = 128
RING = 4
CORES = 2
SIDE = 8
TABLE_PARTS = 16
TABLE_SLOTS = 6
ROUNDS = 4
STRIDE = 27
UNSTRIDE = 19
LOG2E = 1.4426950408889634
LOWEST = -1e30
MESH = pl.DeviceIdType.MESH


def whereabouts():
    tower = lax.axis_index("tower")
    shard = lax.axis_index("shard")
    return tower, shard // 16, shard // 8 % 2, shard // 2 % 4, shard % 2


def shard_at(y, x_hi, z, core):
    return ((y * 2 + x_hi) * 4 + z) * 2 + core


def own_line(position, core=None):
    tower, y, x_hi, z, c = whereabouts()
    c = c if core is None else core
    return shard_at(y + tower * (position - y), x_hi, z + (1 - tower) * (position - z), c)


def cross_line(position):
    tower, y, x_hi, z, c = whereabouts()
    return shard_at(y + (1 - tower) * (position - y), x_hi, z + tower * (position - z), c)


def below_line(position, core):
    tower, y, x_hi, z, _ = whereabouts()
    plane = x_hi * tower + (1 - x_hi) * (1 - tower)
    return shard_at(y + tower * (position - y), plane, z + (1 - tower) * (position - z), core)


def above_line(position, core):
    tower, y, x_hi, z, _ = whereabouts()
    plane = x_hi * (1 - tower) + (1 - x_hi) * tower
    return shard_at(y + (1 - tower) * (position - y), plane, z + tower * (position - z), core)


def hop(i):
    return i + i // 2 - 2 * (i // 3)


def fold(op, parts):
    parts = list(parts)
    while len(parts) > 1:
        odd = parts[len(parts) // 2 * 2 :]
        parts = [op(a, b) for a, b in zip(parts[::2], parts[1::2])] + odd
    return parts[0]


def lane_groups(x):
    return [x[:, q : q + 128] for q in range(0, x.shape[1], 128)]


def sublane_groups(x):
    return [x[r : r + 8] for r in range(0, x.shape[0], 8)]


def remote(src, dst, send, recv, tower, shard):
    return pltpu.make_async_remote_copy(
        src_ref=src, dst_ref=dst, send_sem=send, recv_sem=recv,
        device_id=(tower, shard), device_id_type=MESH,
    )


def arrived(ref, sem):
    pltpu.make_async_copy(ref, ref, sem).wait()


def kernel(
    owner_ref, block_ref, offset_ref, weight_ref, labels_ref, scale_ref, w_in_hbm, w_out_hbm, table_ref,
    out_ref,
    w_in_ref, w_out_ref, table_16, table_32, ask, relay, asked, asked_at, staged, outgoing, fetched,
    mix_high, mix_low, pooled_sum, pooled_16,
    emb, own, other, own_labels, other_labels, score_even, score_odd, row_key, col_key,
    row_max, row_sum, row_hit, col_max, col_sum, col_hit, row_note, col_note, row_post, col_post,
    weight_sem, table_sem, near_send, near_recv, far_send, far_recv, asked_sem, rows_send, rows_recv,
    own_label_send, own_label_recv, other_label_send, other_label_recv,
    own_send, own_recv, down_send, cross_send, swap_send, other_recv,
    row_send, row_recv, col_send, col_recv,
):
    f32, bf16 = jnp.float32, jnp.bfloat16
    bag, rows = owner_ref.shape
    groups, lanes = SIDE * SIDE, ask.shape[3]
    capacity = outgoing.shape[0] // groups
    tower, y, x_hi, z, core = whereabouts()
    me = lax.axis_index("shard")
    far, near = me // SIDE, me % SIDE
    mine = z + tower * (y - z)
    cross = y + tower * (z - y)

    part = table_16.shape[1]
    loads = []
    for i in range(TABLE_PARTS):
        at = pl.ds(i * part, part)
        loads.append(pltpu.make_async_copy(table_ref.at[at], table_16.at[i % TABLE_SLOTS], table_sem.at[i]))
    weight_loads = [
        pltpu.make_async_copy(w_in_hbm, w_in_ref, weight_sem.at[0]),
        pltpu.make_async_copy(w_out_hbm, w_out_ref, weight_sem.at[1]),
    ]
    for load in loads[:TABLE_SLOTS]:
        load.start()

    barrier = pltpu.get_barrier_semaphore()

    def greet(tower_id, shard_id):
        pl.semaphore_signal(barrier, inc=1, device_id=(tower_id, shard_id), device_id_type=MESH)

    for step in range(1, SIDE):
        greet(tower, far * SIDE + (near + step) % SIDE)
        greet(tower, (far + step) % SIDE * SIDE + near)
    for p in range(RING):
        for c in range(CORES):
            greet(1 - tower, below_line(p, c))
            greet(1 - tower, above_line(p, c))

    group = lax.broadcasted_iota(jnp.int32, (groups, rows), 0)
    all_owners = owner_ref[...]
    step_y = (y + RING - lax.shift_right_logical(all_owners, 4)) & 3
    step_x = (x_hi + 2 - (lax.shift_right_logical(all_owners, 3) & 1)) & 1
    step_z = (z + RING - (lax.shift_right_logical(all_owners, 1) & 3)) & 3
    step_c = (core + 2 - (all_owners & 1)) & 1
    turn = (((step_y * 2 + step_x) * 4 + step_z) * 2 + step_c) * UNSTRIDE & (groups - 1)
    first_slot = (turn * capacity).astype(f32)
    named = [all_owners[k : k + 1, :] == group for k in range(bag)]
    count = sum(jnp.where(n, 1.0, 0.0) for n in named)
    before = jnp.where(
        lax.broadcasted_iota(jnp.int32, (rows, rows), 0) < lax.broadcasted_iota(jnp.int32, (rows, rows), 1),
        1.0, 0.0).astype(bf16)
    place = jnp.dot(count.astype(bf16), before, preferred_element_type=f32)
    lane_of = lax.broadcasted_iota(jnp.int32, (lanes, rows), 0).astype(f32)
    wanted = jnp.zeros((2 * groups, lanes), f32)
    slots = []
    for k in range(bag):
        slot = jnp.sum(jnp.where(named[k], place, 0.0), axis=0, keepdims=True)
        block = jnp.where(named[k], block_ref[k : k + 1, :].astype(f32), 0.0)
        offset = jnp.where(named[k], offset_ref[k : k + 1, :].astype(f32), 0.0)
        taken = jnp.where(lane_of == slot, 1.0, 0.0).astype(bf16)
        wanted += lax.dot_general(jnp.concatenate([block, offset], axis=0).astype(bf16), taken,
                                  (((1,), (1,)), ((), ())), preferred_element_type=f32)
        slots.append(slot)
    wanted = (wanted[:groups] * ROW_BLOCK + wanted[groups:]).astype(jnp.int32)
    wanted = jnp.clip(wanted, 0, table_32.shape[0] - 1)
    for g in range(groups):
        ask[g % SIDE, g // SIDE] = wanted[g : g + 1]

    pl.semaphore_wait(barrier, 2 * (SIDE - 1) + 2 * RING * CORES)

    def near_request(step):
        to = (near + step) % SIDE
        return remote(ask.at[to], relay.at[near], near_send.at[step], near_recv.at[near],
                      tower, far * SIDE + to)

    def far_request(step):
        to = (far + step) % SIDE
        return remote(relay.at[:, to], asked.at[far], far_send.at[step], far_recv.at[far],
                      tower, to * SIDE + near)

    for step in range(1, SIDE):
        near_request(step).start()
    relay[near] = ask[near]

    def widen(i):
        loads[i].wait()

        def some(j, carry):
            to = pl.ds(pl.multiple_of(i * part + j * 128, 128), 128)
            at = pl.ds(pl.multiple_of(j * 128, 128), 128)
            table_32[to] = table_16[i % TABLE_SLOTS, at].astype(f32)
            return carry

        lax.fori_loop(0, part // 128, some, 0)
        if i + TABLE_SLOTS < TABLE_PARTS:
            loads[i + TABLE_SLOTS].start()

    for i in range(TABLE_PARTS // 2):
        widen(i)
    for step in range(1, SIDE):
        p = (near + step) % SIDE
        arrived(relay.at[p], near_recv.at[p])
    for step in range(1, SIDE):
        far_request(step).start()
    asked[far] = relay[:, far]
    for i in range(TABLE_PARTS // 2, TABLE_PARTS):
        widen(i)
    for step in range(1, SIDE):
        p = (far + step) % SIDE
        arrived(asked.at[p], far_recv.at[p])
    for load in weight_loads:
        load.start()
    to_scalar = pltpu.make_async_copy(asked, asked_at, asked_sem)
    to_scalar.start()
    to_scalar.wait()

    def partner(i):
        step = i * STRIDE % groups
        return shard_at((y + step // 16) % 4, (x_hi + step // 8) % 2, (z + step // 2) % 4,
                        (core + step) % 2)

    def block_of(ref, i):
        return ref.at[pl.ds(pl.multiple_of(i * capacity, 16), capacity)]

    def look_up(p, destination):
        for c in range(capacity):
            row = jnp.clip(asked_at[p // SIDE, p % SIDE, 0, c], 0, table_32.shape[0] - 1)
            staged[c : c + 1] = table_32[pl.ds(row, 1)]
        destination[...] = staged[...].astype(bf16)

    def serve(i, carry):
        p = partner(i)
        block = block_of(outgoing, i)
        look_up(p, block)
        remote(block, block_of(fetched, i), rows_send, rows_recv.at[i // (groups // ROUNDS)], tower, p).start()
        return carry

    lax.fori_loop(1, groups, serve, 0)
    look_up(me, block_of(fetched, 0))

    def own_label(step):
        return remote(labels_ref, own_labels.at[mine], own_label_send.at[step], own_label_recv.at[mine],
                      tower, own_line((mine + step) % RING))

    def other_label(p, c):
        return remote(labels_ref, other_labels.at[mine, core], other_label_send.at[p, c],
                      other_label_recv.at[mine, core], 1 - tower, below_line(p, c))

    for step in range(1, RING):
        own_label(step).start()
    for p in range(RING):
        for c in range(CORES):
            other_label(p, c).start()
    own_labels[mine] = labels_ref[...]

    target_wide, weight_wide = score_even, score_odd
    for k in range(bag):
        target_wide[:, k * lanes : (k + 1) * lanes] = jnp.transpose(
            jnp.broadcast_to(first_slot[k : k + 1, :] + slots[k], (lanes, rows)))
        weight_wide[:, k * lanes : (k + 1) * lanes] = jnp.transpose(jnp.broadcast_to(weight_ref[k : k + 1, :], (lanes, rows)))
    lane = lax.broadcasted_iota(jnp.int32, (16, lanes), 1).astype(f32)
    spread = mix_high.shape[1] // lanes

    def weigh(i, carry):
        at = pl.ds(pl.multiple_of(i * 16, 16), 16)
        targets = [target_wide[at, k * lanes : (k + 1) * lanes] for k in range(bag)]
        weights = [weight_wide[at, k * lanes : (k + 1) * lanes] for k in range(bag)]

        def column(j, carry):
            here = lane + (j * lanes).astype(f32)
            mixed = jnp.zeros((16, lanes), f32)
            for k in range(bag):
                mixed = jnp.where(targets[k] == here, weights[k], mixed)
            high = mixed.astype(bf16)
            cols = pl.ds(pl.multiple_of(j * lanes, lanes), lanes)
            mix_high[at, cols] = high
            mix_low[at, cols] = (mixed - high.astype(f32)).astype(bf16)
            return carry

        return lax.fori_loop(0, spread, column, carry, unroll=4)

    lax.fori_loop(0, rows // 16, weigh, 0)

    for step in range(1, RING):
        p = (mine + step) % RING
        arrived(own_labels.at[p], own_label_recv.at[p])
    for p in range(RING):
        for c in range(CORES):
            arrived(other_labels.at[p, c], other_label_recv.at[p, c])
    number = lax.broadcasted_iota(jnp.int32, (1, rows), 1)
    for p in range(RING):
        key = jnp.where(tower == 0, own_labels[p], own_line(p) * rows + number)
        row_key[p] = jnp.transpose(jnp.broadcast_to(key, (128, rows)))
        col_key[p] = jnp.concatenate(
            [jnp.where(tower == 0, above_line(p, c) * rows + number, other_labels[p, c]) for c in range(CORES)],
            axis=1)
    row_max[...] = jnp.full(row_max.shape, LOWEST, f32)
    col_max[...] = jnp.full(col_max.shape, LOWEST, f32)
    for ref in (row_sum, row_hit, col_sum, col_hit):
        ref[...] = jnp.zeros(ref.shape, f32)

    sources = groups // ROUNDS
    deep = sources * capacity
    pooled_sum[...] = jnp.zeros(pooled_sum.shape, f32)
    for i in range(ROUNDS):
        first = capacity if i == 0 else i * deep
        landed = fetched.at[pl.ds(first, (i + 1) * deep - first)]
        arrived(landed, rows_recv.at[i])
        at = slice(i * deep, (i + 1) * deep)
        data = fetched[at]
        pooled_sum[...] += (
            jnp.dot(mix_high[:, at], data, preferred_element_type=f32)
            + jnp.dot(mix_low[:, at], data, preferred_element_type=f32))
    pooled_16[...] = pooled_sum[...].astype(bf16)
    pooled_sum[...] = pooled_16[...].astype(f32)
    for load in weight_loads:
        load.wait()
    hidden_part = 256

    def layer(i, carry):
        at = pl.ds(pl.multiple_of(i * hidden_part, hidden_part), hidden_part)
        v = jnp.dot(pooled_16[...], w_in_ref[:, at], preferred_element_type=f32)
        hidden = (v / (1.0 + jnp.exp(-v))).astype(bf16)
        pooled_sum[...] += jnp.dot(hidden, w_out_ref[at, :], preferred_element_type=f32)
        return carry

    lax.fori_loop(0, w_in_ref.shape[1] // hidden_part, layer, 0, unroll=2)
    widened = pooled_sum[...]
    emb[...] = (widened * lax.rsqrt(jnp.sum(widened * widened, axis=1, keepdims=True) + 1e-06)).astype(bf16)

    def half(c):
        return pl.ds(pl.multiple_of(c * rows, rows), rows)

    def down():
        return remote(emb, other.at[mine, half(core)], down_send, other_recv.at[mine, core],
                      1 - tower, below_line(mine, core))

    def along(step):
        return remote(emb, own.at[mine], own_send.at[step], own_recv.at[mine],
                      tower, own_line((mine + step) % RING))

    def across(step):
        here = other.at[cross, half(core)]
        return remote(here, here, cross_send.at[step], other_recv.at[cross, core],
                      tower, cross_line((cross + step) % RING))

    def swap(p):
        here = other.at[p, half(core)]
        return remote(here, here, swap_send.at[p], other_recv.at[p, core], tower, own_line(mine, 1 - core))

    def other_arrived(p, c):
        arrived(other.at[p, half(c)], other_recv.at[p, c])

    def own_arrived(step):
        p = (mine + step) % RING
        arrived(own.at[p], own_recv.at[p])

    down().start()
    along(1).start()
    along(3).start()
    own[mine] = emb[...]
    other_arrived(cross, core)
    swap(cross).start()
    across(1).start()
    across(3).start()
    along(2).start()
    own_arrived(1)
    own_arrived(3)
    across(2).start()
    other_arrived(cross, 1 - core)

    scale = scale_ref[0, 0]
    to_log2 = scale * LOG2E
    strip = 16

    def product(step, destination):
        p = (cross + hop(step // RING)) % RING
        a = (mine + hop(step % RING)) % RING
        destination[...] = lax.dot_general(own[a], other[p], (((1,), (1,)), ((), ())),
                                           preferred_element_type=f32)

    def gather_sums(step, source):
        p = (cross + hop(step // RING)) % RING
        a = (mine + hop(step % RING)) % RING
        col_old = col_max[p]

        def tops(r, carry):
            at = pl.ds(r * strip, strip)
            s = source[at]
            old = row_max[a, at]
            new = jnp.maximum(old, fold(jnp.maximum, lane_groups(s)))
            row_sum[a, at] = row_sum[a, at] * jnp.exp2((old - new) * to_log2)
            row_max[a, at] = new
            return jnp.maximum(carry, fold(jnp.maximum, sublane_groups(s)))

        col_new = lax.fori_loop(0, rows // strip, tops, col_old, unroll=True)
        col_max[p] = col_new
        col_top = col_new * to_log2
        key = col_key[p]

        def sums(r, carry):
            c_sum, c_hit = carry
            at = pl.ds(r * strip, strip)
            r_top = row_max[a, at] * to_log2
            r_sum, r_hit, r_key = row_sum[a, at], row_hit[a, at], row_key[a, at]
            new_sum, new_hit = [], []
            for q in range(0, CORES * rows, 128):
                group = slice(q, q + 128)
                s = source[at, group]
                t = s * to_log2
                r_sum = r_sum + jnp.exp2(t - r_top)
                e = jnp.exp2(t - jnp.concatenate([col_top[:, group]] * (strip // 8), axis=0))
                new_sum.append(c_sum[:, group] + fold(jnp.add, sublane_groups(e)))
                positive = r_key == jnp.broadcast_to(key[:, group], (strip, 128))
                r_hit = jnp.where(positive, s, r_hit)
                hit = c_hit[:, group]
                for v in range(0, strip, 8):
                    here = r_key[v : v + 8] == jnp.broadcast_to(key[:, group], (8, 128))
                    hit = jnp.where(here, s[v : v + 8], hit)
                new_hit.append(hit)
            row_sum[a, at] = r_sum
            row_hit[a, at] = r_hit
            return jnp.concatenate(new_sum, axis=1), jnp.concatenate(new_hit, axis=1)

        start = (col_sum[p] * jnp.exp2(col_old * to_log2 - col_top), col_hit[p])
        c_sum, c_hit = lax.fori_loop(0, rows // strip, sums, start, unroll=True)
        col_sum[p] = c_sum
        col_hit[p] = c_hit

    def send_col_note(p, c):
        return remote(col_note.at[p, c], col_post.at[cross, core], col_send.at[p, c], col_recv.at[cross, core],
                      1 - tower, above_line(p, c))

    last = RING * RING - 1
    product(0, score_even)

    def pieces(j, carry):
        @pl.when(j == 1)
        def _():
            own_arrived(2)

        for when, index in ((1, 1), (2, 2), (4, 3)):
            @pl.when(j == when)
            def _(index=index):
                p = (cross + hop(index)) % RING
                other_arrived(p, core)
                swap(p).start()

        for when, index in ((1, 1), (3, 2), (5, 3)):
            @pl.when(j == when)
            def _(index=index):
                other_arrived((cross + hop(index)) % RING, 1 - core)

        product(2 * j + 1, score_odd)
        gather_sums(2 * j, score_even)
        product(jnp.minimum(2 * j + 2, last), score_even)
        gather_sums(2 * j + 1, score_odd)

        @pl.when(j % 2 == 1)
        def _():
            p = (cross + hop(j // 2)) % RING
            top = jnp.max(col_max[p], axis=0, keepdims=True)
            total = jnp.sum(col_sum[p] * jnp.exp2((col_max[p] - top) * to_log2), axis=0, keepdims=True)
            hit = jnp.sum(col_hit[p], axis=0, keepdims=True)
            for c in range(CORES):
                for n, value in enumerate((top, total, hit)):
                    col_note[p, c, n] = value[:, c * rows : (c + 1) * rows]
                send_col_note(p, c).start()

        return carry

    lax.fori_loop(0, RING * RING // 2, pieces, 0)

    wide_lane = lax.broadcasted_iota(jnp.int32, (rows, 128), 1)

    def send_row_note(step):
        p = (mine + step) % RING
        return remote(row_note.at[p], row_post.at[mine], row_send.at[step], row_recv.at[mine],
                      tower, own_line(p))

    def row_totals(a):
        top = jnp.max(row_max[a], axis=1, keepdims=True)
        total = jnp.sum(row_sum[a] * jnp.exp2((row_max[a] - top) * to_log2), axis=1, keepdims=True)
        hit = jnp.sum(row_hit[a], axis=1, keepdims=True)
        packed = jnp.where(wide_lane == 0, top, jnp.where(wide_lane == 1, total, hit))
        packed = jnp.transpose(packed)
        for n in range(3):
            row_note[a, n] = packed[n : n + 1]

    def row_results(i, carry):
        step = i + 1
        row_totals((mine + step) % RING)
        send_row_note(step).start()
        return carry

    lax.fori_loop(0, RING - 1, row_results, 0)
    row_totals(mine)
    notes = [[row_note[mine, n] for n in range(3)]]
    for p in range(RING):
        for c in range(CORES):
            arrived(col_post.at[p, c], col_recv.at[p, c])
            notes.append([col_post[p, c, n] for n in range(3)])
    for step in (1, 2, 3):
        p = (mine + step) % RING
        arrived(row_post.at[p], row_recv.at[p])
        notes.append([row_post[p, n] for n in range(3)])
    top = fold(jnp.maximum, [n[0] for n in notes])
    total = fold(jnp.add, [n[1] * jnp.exp2((n[0] - top) * to_log2) for n in notes])
    hit = fold(jnp.add, [n[2] for n in notes])
    out_ref[...] = scale * (top - hit) + jnp.log(total)

    for step in range(1, SIDE):
        near_request(step).wait_send()
        far_request(step).wait_send()
    gone = outgoing.at[pl.ds(capacity, (groups - 1) * capacity)]
    arrived(gone, rows_send)
    for step in range(1, RING):
        own_label(step).wait_send()
        along(step).wait_send()
        across(step).wait_send()
        send_row_note(step).wait_send()
    down().wait_send()
    for p in range(RING):
        swap(p).wait_send()
        for c in range(CORES):
            other_label(p, c).wait_send()
            send_col_note(p, c).wait_send()


def tower_losses(table, owner, block, offset, weight, w_in, w_out, labels, logit_scale):
    bag, rows = owner.shape
    groups = lax.axis_size("shard")
    capacity = 8 * ((5 * bag * rows + 32 * groups - 1) // (32 * groups))
    width = table.shape[1]
    lanes = 128
    f32, bf16, i32 = jnp.float32, jnp.bfloat16, jnp.int32
    dma = pltpu.SemaphoreType.DMA
    slots = groups * capacity
    vmem = pl.BlockSpec(memory_space=pltpu.VMEM)
    anywhere = pl.BlockSpec(memory_space=pl.ANY)
    return pl.pallas_call(
        kernel,
        out_shape=jax.ShapeDtypeStruct((1, rows), f32),
        in_specs=[vmem] * 5 + [pl.BlockSpec(memory_space=pltpu.SMEM)] + [anywhere] * 3,
        out_specs=vmem,
        scratch_shapes=[
            pltpu.VMEM(w_in.shape, bf16),
            pltpu.VMEM(w_out.shape, bf16),
            pltpu.VMEM((TABLE_SLOTS, table.shape[0] // TABLE_PARTS, width), bf16),
            pltpu.VMEM(table.shape, f32),
            pltpu.VMEM((SIDE, SIDE, 1, lanes), i32),
            pltpu.VMEM((SIDE, SIDE, 1, lanes), i32),
            pltpu.VMEM((SIDE, SIDE, 1, lanes), i32),
            pltpu.SMEM((SIDE, SIDE, 1, lanes), i32),
            pltpu.VMEM((capacity, width), f32),
            pltpu.VMEM((slots, width), bf16),
            pltpu.VMEM((slots, width), bf16),
            pltpu.VMEM((rows, slots), bf16),
            pltpu.VMEM((rows, slots), bf16),
            pltpu.VMEM((rows, width), f32),
            pltpu.VMEM((rows, width), bf16),
            pltpu.VMEM((rows, width), bf16),
            pltpu.VMEM((RING, rows, width), bf16),
            pltpu.VMEM((RING, CORES * rows, width), bf16),
            pltpu.VMEM((RING, 1, rows), i32),
            pltpu.VMEM((RING, CORES, 1, rows), i32),
            pltpu.VMEM((rows, CORES * rows), f32),
            pltpu.VMEM((rows, CORES * rows), f32),
            pltpu.VMEM((RING, rows, 128), i32),
            pltpu.VMEM((RING, 1, CORES * rows), i32),
            pltpu.VMEM((RING, rows, 128), f32),
            pltpu.VMEM((RING, rows, 128), f32),
            pltpu.VMEM((RING, rows, 128), f32),
            pltpu.VMEM((RING, 8, CORES * rows), f32),
            pltpu.VMEM((RING, 8, CORES * rows), f32),
            pltpu.VMEM((RING, 8, CORES * rows), f32),
            pltpu.VMEM((RING, 3, 1, rows), f32),
            pltpu.VMEM((RING, CORES, 3, 1, rows), f32),
            pltpu.VMEM((RING, 3, 1, rows), f32),
            pltpu.VMEM((RING, CORES, 3, 1, rows), f32),
            dma((2,)), dma((TABLE_PARTS,)), dma((SIDE,)), dma((SIDE,)), dma((SIDE,)), dma((SIDE,)),
            dma, dma, dma((ROUNDS,)),
            dma((RING,)), dma((RING,)), dma((RING, CORES)), dma((RING, CORES)),
            dma((RING,)), dma((RING,)), dma, dma((RING,)), dma((RING,)), dma((RING, CORES)),
            dma((RING,)), dma((RING,)), dma((RING, CORES)), dma((RING, CORES)),
        ],
        compiler_params=pltpu.CompilerParams(
            collective_id=1, has_side_effects=True, vmem_limit_bytes=61 * 1024 * 1024
        ),
        cost_estimate=pl.CostEstimate(
            flops=2 * 2048 * 4096 * width, bytes_accessed=2 * table.size, transcendentals=4 * 2048 * 4096
        ),
        name="tower_losses",
    )(owner, block, offset, weight, labels.reshape(1, rows), logit_scale.reshape(1, 1), w_in, w_out, table)


def per_device(
    tables, bag_owner, bag_block, bag_offset, bag_weight, w_in, w_out, labels, logit_scale
):
    return tower_losses(
        tables[0], bag_owner[0].T, bag_block[0].T, bag_offset[0].T, bag_weight[0].T, w_in[0], w_out[0],
        labels, logit_scale,
    )


def solution(mesh):
    placed = (
        P("tower", "shard", None),
        P("tower", "shard", None),
        P("tower", "shard", None),
        P("tower", "shard", None),
        P("tower", "shard", None),
        P("tower", None, None),
        P("tower", None, None),
        P("shard"),
        P(),
    )
    return jax.shard_map(
        per_device, mesh=mesh, in_specs=placed, out_specs=P("tower", "shard"), check_vma=False
    )
```

time: 357 us -> 105 us (0.29)
  the two profiles are of different devices: /device:TPU:1 before, /device:TPU:33 now
where the time goes in v2:
time: 105 us; the launch traced here: 104 us
  Pallas kernels  103 us (98%)
  local copies, waits for them, and re-layouts  1.26 us (1%)
    pallas_call x1, Pallas kernels, tower_losses(): pl.pallas_call(kernel, out_shape=jax.ShapeDtypeStruct((1, rows), f32), in...  103 us

profile of v2, /device:TPU:33, one launch (start us, length us, event | category | flops | bytes accessed | tf_op | source)
XLA Modules:
  0.0 104.5 jit_solution(15993314632069747769)
XLA Ops:
  0.7 102.6 %tower_losses.1 = f32[1,512]{1,0:T(1,128)} custom-call(s32[8,512]{1,0:T(8,128)} %bitcast.21, s32[8,512]{1,0:T(8,128)} %bitcast.22, s32[8,512]{1,0:T(8,128)} %bitcast.23, f32[8,512]{1,0:T(8,128)} %bitcast.24, s32[1,512]{1,0:T(1,128)} %bitcast.25, f32[1,1]{1,0:T(1,128)} %bitcast.17.scale_ref, bf16[256,2048]{1,0:T(8,128)(2,1)} %bitcast.19, ...), custom_call_target="tpu_custom_call" | custom-call | flops 4294967296 | bytes 8388608 | tf_op jit(solution)/shard_map/tower_losses/pallas_call | solution.py:535
  103.2 1.3 %copy.12 = f32[1,512]{1,0:T(1,128)} copy(f32[1,512]{1,0:T(1,128)} %tower_losses.1) | data formatting | bytes 4096

commit v3 on v2

--- a/solution.py
+++ b/solution.py
@@ -12,8 +12,8 @@
 TABLE_PARTS = 16
 TABLE_SLOTS = 6
 ROUNDS = 4
-STRIDE = 27
-UNSTRIDE = 19
+TURNS = SIDE * SIDE // ROUNDS
+FIRST = 2 * SIDE - 1
 LOG2E = 1.4426950408889634
 LOWEST = -1e30
 MESH = pl.DeviceIdType.MESH
@@ -86,18 +86,18 @@
 def kernel(
     owner_ref, block_ref, offset_ref, weight_ref, labels_ref, scale_ref, w_in_hbm, w_out_hbm, table_ref,
     out_ref,
-    w_in_ref, w_out_ref, table_16, table_32, ask, relay, asked, asked_at, staged, outgoing, fetched,
+    w_in_ref, w_out_ref, table_16, table_32, ask, asked, asked_at, staged, outgoing, fetched,
     mix_high, mix_low, pooled_sum, pooled_16,
     emb, own, other, own_labels, other_labels, score_even, score_odd, row_key, col_key,
     row_max, row_sum, row_hit, col_max, col_sum, col_hit, row_note, col_note, row_post, col_post,
-    weight_sem, table_sem, near_send, near_recv, far_send, far_recv, asked_sem, rows_send, rows_recv,
+    weight_sem, table_sem, known, ask_send, ask_recv, asked_sem, rows_send, rows_recv,
     own_label_send, own_label_recv, other_label_send, other_label_recv,
     own_send, own_recv, down_send, cross_send, swap_send, other_recv,
     row_send, row_recv, col_send, col_recv,
 ):
     f32, bf16 = jnp.float32, jnp.bfloat16
     bag, rows = owner_ref.shape
-    groups, lanes = SIDE * SIDE, ask.shape[3]
+    groups, lanes = SIDE * SIDE, ask.shape[2]
     capacity = outgoing.shape[0] // groups
     tower, y, x_hi, z, core = whereabouts()
     me = lax.axis_index("shard")
@@ -125,18 +125,17 @@
     for step in range(1, SIDE):
         greet(tower, far * SIDE + (near + step) % SIDE)
         greet(tower, (far + step) % SIDE * SIDE + near)
-    for p in range(RING):
-        for c in range(CORES):
-            greet(1 - tower, below_line(p, c))
-            greet(1 - tower, above_line(p, c))
+    greet(1 - tower, below_line(mine, core))
+    greet(1 - tower, above_line(cross, core))
 
     group = lax.broadcasted_iota(jnp.int32, (groups, rows), 0)
     all_owners = owner_ref[...]
-    step_y = (y + RING - lax.shift_right_logical(all_owners, 4)) & 3
-    step_x = (x_hi + 2 - (lax.shift_right_logical(all_owners, 3) & 1)) & 1
-    step_z = (z + RING - (lax.shift_right_logical(all_owners, 1) & 3)) & 3
-    step_c = (core + 2 - (all_owners & 1)) & 1
-    turn = (((step_y * 2 + step_x) * 4 + step_z) * 2 + step_c) * UNSTRIDE & (groups - 1)
+    step_far = (lax.shift_right_logical(all_owners, 3) + SIDE - far) & (SIDE - 1)
+    step_near = (all_owners + SIDE - near) & (SIDE - 1)
+    diagonal = step_near - step_far
+    diagonal = jnp.where(diagonal < 0, diagonal + SIDE - 1, diagonal)
+    turn = FIRST + (SIDE - 1) * diagonal + step_far - 1
+    turn = jnp.where(step_far == 0, step_near, jnp.where(step_near == 0, SIDE - 1 + step_far, turn))
     first_slot = (turn * capacity).astype(f32)
     named = [all_owners[k : k + 1, :] == group for k in range(bag)]
     count = sum(jnp.where(n, 1.0, 0.0) for n in named)
@@ -158,24 +157,29 @@
     wanted = (wanted[:groups] * ROW_BLOCK + wanted[groups:]).astype(jnp.int32)
     wanted = jnp.clip(wanted, 0, table_32.shape[0] - 1)
     for g in range(groups):
-        ask[g % SIDE, g // SIDE] = wanted[g : g + 1]
-
-    pl.semaphore_wait(barrier, 2 * (SIDE - 1) + 2 * RING * CORES)
-
-    def near_request(step):
-        to = (near + step) % SIDE
-        return remote(ask.at[to], relay.at[near], near_send.at[step], near_recv.at[near],
-                      tower, far * SIDE + to)
-
-    def far_request(step):
-        to = (far + step) % SIDE
-        return remote(relay.at[:, to], asked.at[far], far_send.at[step], far_recv.at[far],
-                      tower, to * SIDE + near)
+        ask[g] = wanted[g : g + 1]
+
+    pl.semaphore_wait(barrier, 2 * SIDE)
 
     for step in range(1, SIDE):
-        near_request(step).start()
-    relay[near] = ask[near]
-
+        pl.semaphore_signal(known, inc=1, device_id=(tower, (far + step) % SIDE * SIDE + near),
+                            device_id_type=MESH)
+
+    def neighbour(step_far, step_near):
+        return (far + step_far) % SIDE * SIDE + (near + step_near) % SIDE
+
+    def later_steps(i):
+        later = i - FIRST
+        return 1 + later % (SIDE - 1), 1 + (later + later // (SIDE - 1)) % (SIDE - 1)
+
+    def request(i, to):
+        return remote(ask.at[to], asked.at[i], ask_send, ask_recv.at[i // TURNS], tower, to)
+
+    for i in range(1, SIDE):
+        request(i, neighbour(0, i)).start()
+    for i in range(1, SIDE):
+        request(SIDE - 1 + i, neighbour(i, 0)).start()
+    asked[0] = ask[me]
     def widen(i):
         loads[i].wait()
 
@@ -189,56 +193,72 @@
         if i + TABLE_SLOTS < TABLE_PARTS:
             loads[i + TABLE_SLOTS].start()
 
+    def send_requests(first, end):
+        def send(i, carry):
+            request(i, neighbour(*later_steps(i))).start()
+            return carry
+
+        lax.fori_loop(first, end, send, 0)
+
     for i in range(TABLE_PARTS // 2):
         widen(i)
-    for step in range(1, SIDE):
-        p = (near + step) % SIDE
-        arrived(relay.at[p], near_recv.at[p])
-    for step in range(1, SIDE):
-        far_request(step).start()
-    asked[far] = relay[:, far]
+    pl.semaphore_wait(known, SIDE - 1)
+    send_requests(FIRST, TURNS)
     for i in range(TABLE_PARTS // 2, TABLE_PARTS):
         widen(i)
-    for step in range(1, SIDE):
-        p = (far + step) % SIDE
-        arrived(asked.at[p], far_recv.at[p])
     for load in weight_loads:
         load.start()
-    to_scalar = pltpu.make_async_copy(asked, asked_at, asked_sem)
-    to_scalar.start()
-    to_scalar.wait()
-
-    def partner(i):
-        step = i * STRIDE % groups
-        return shard_at((y + step // 16) % 4, (x_hi + step // 8) % 2, (z + step // 2) % 4,
-                        (core + step) % 2)
 
     def block_of(ref, i):
         return ref.at[pl.ds(pl.multiple_of(i * capacity, 16), capacity)]
 
-    def look_up(p, destination):
+    def look_up(i, destination):
         for c in range(capacity):
-            row = jnp.clip(asked_at[p // SIDE, p % SIDE, 0, c], 0, table_32.shape[0] - 1)
+            row = jnp.clip(asked_at[i, 0, c], 0, table_32.shape[0] - 1)
             staged[c : c + 1] = table_32[pl.ds(row, 1)]
         destination[...] = staged[...].astype(bf16)
 
-    def serve(i, carry):
-        p = partner(i)
+    def serve(i, to):
         block = block_of(outgoing, i)
-        look_up(p, block)
-        remote(block, block_of(fetched, i), rows_send, rows_recv.at[i // (groups // ROUNDS)], tower, p).start()
+        look_up(i, block)
+        remote(block, block_of(fetched, i), rows_send, rows_recv.at[i // TURNS], tower, to).start()
+
+    def serve_near(i, carry):
+        serve(i, neighbour(0, SIDE - i))
         return carry
 
-    lax.fori_loop(1, groups, serve, 0)
-    look_up(me, block_of(fetched, 0))
+    def serve_far(i, carry):
+        serve(i, neighbour(FIRST - i, 0))
+        return carry
+
+    def serve_later(i, carry):
+        step_far, step_near = later_steps(i)
+        serve(i, neighbour(SIDE - step_far, SIDE - step_near))
+        return carry
+
+    for n in range(ROUNDS):
+        first, end = max(n * TURNS, 1), (n + 1) * TURNS
+        arrived(asked.at[pl.ds(first, end - first)], ask_recv.at[n])
+        to_scalar = pltpu.make_async_copy(
+            asked.at[pl.ds(n * TURNS, TURNS)], asked_at.at[pl.ds(n * TURNS, TURNS)], asked_sem)
+        to_scalar.start()
+        if n + 1 < ROUNDS:
+            send_requests(end, end + TURNS)
+        to_scalar.wait()
+        if n == 0:
+            lax.fori_loop(SIDE, FIRST, serve_far, 0)
+            lax.fori_loop(1, SIDE, serve_near, 0)
+            first = FIRST
+        lax.fori_loop(first, end, serve_later, 0)
+    look_up(0, block_of(fetched, 0))
 
     def own_label(step):
         return remote(labels_ref, own_labels.at[mine], own_label_send.at[step], own_label_recv.at[mine],
                       tower, own_line((mine + step) % RING))
 
     def other_label(p, c):
-        return remote(labels_ref, other_labels.at[mine, core], other_label_send.at[p, c],
-                      other_label_recv.at[mine, core], 1 - tower, below_line(p, c))
+        return remote(labels_ref, other_labels.at[z, core], other_label_send.at[p, c],
+                      other_label_recv.at[z, core], tower, shard_at(y, 1 - x_hi, p, c))
 
     for step in range(1, RING):
         own_label(step).start()
@@ -293,8 +313,7 @@
     for ref in (row_sum, row_hit, col_sum, col_hit):
         ref[...] = jnp.zeros(ref.shape, f32)
 
-    sources = groups // ROUNDS
-    deep = sources * capacity
+    deep = TURNS * capacity
     pooled_sum[...] = jnp.zeros(pooled_sum.shape, f32)
     for i in range(ROUNDS):
         first = capacity if i == 0 else i * deep
@@ -310,58 +329,80 @@
     for load in weight_loads:
         load.wait()
     hidden_part = 256
-
-    def layer(i, carry):
-        at = pl.ds(pl.multiple_of(i * hidden_part, hidden_part), hidden_part)
-        v = jnp.dot(pooled_16[...], w_in_ref[:, at], preferred_element_type=f32)
-        hidden = (v / (1.0 + jnp.exp(-v))).astype(bf16)
-        pooled_sum[...] += jnp.dot(hidden, w_out_ref[at, :], preferred_element_type=f32)
-        return carry
-
-    lax.fori_loop(0, w_in_ref.shape[1] // hidden_part, layer, 0, unroll=2)
-    widened = pooled_sum[...]
-    emb[...] = (widened * lax.rsqrt(jnp.sum(widened * widened, axis=1, keepdims=True) + 1e-06)).astype(bf16)
-
-    def half(c):
-        return pl.ds(pl.multiple_of(c * rows, rows), rows)
-
-    def down():
-        return remote(emb, other.at[mine, half(core)], down_send, other_recv.at[mine, core],
-                      1 - tower, below_line(mine, core))
-
-    def along(step):
-        return remote(emb, own.at[mine], own_send.at[step], own_recv.at[mine],
+    piece = rows // 2
+
+    def some(h, c=0):
+        return pl.ds(pl.multiple_of(c * rows, rows) + h * piece, piece)
+
+    def down(h):
+        return remote(emb.at[some(h)], other.at[mine, some(h, core)], down_send.at[h],
+                      other_recv.at[mine, core, h], 1 - tower, below_line(mine, core))
+
+    def along(step, h):
+        return remote(emb.at[some(h)], own.at[mine, some(h)], own_send.at[step, h], own_recv.at[mine, h],
                       tower, own_line((mine + step) % RING))
 
-    def across(step):
-        here = other.at[cross, half(core)]
-        return remote(here, here, cross_send.at[step], other_recv.at[cross, core],
+    def along_on(h):
+        p = (mine + 3 - 2 * h) % RING
+        here = own.at[p, some(h)]
+        return remote(here, here, own_send.at[2, h], own_recv.at[p, h],
+                      tower, own_line((mine + 1 + 2 * h) % RING))
+
+    def across(step, h):
+        here = other.at[cross, some(h, core)]
+        return remote(here, here, cross_send.at[step, h], other_recv.at[cross, core, h],
                       tower, cross_line((cross + step) % RING))
 
-    def swap(p):
-        here = other.at[p, half(core)]
-        return remote(here, here, swap_send.at[p], other_recv.at[p, core], tower, own_line(mine, 1 - core))
-
-    def other_arrived(p, c):
-        arrived(other.at[p, half(c)], other_recv.at[p, c])
-
-    def own_arrived(step):
+    def across_on(h):
+        p = (cross + 3 - 2 * h) % RING
+        here = other.at[p, some(h, core)]
+        return remote(here, here, cross_send.at[2, h], other_recv.at[p, core, h],
+                      tower, cross_line((cross + 1 + 2 * h) % RING))
+
+    def swap(p, h):
+        here = other.at[p, some(h, core)]
+        return remote(here, here, swap_send.at[p, h], other_recv.at[p, core, h],
+                      tower, own_line(mine, 1 - core))
+
+    def other_arrived(p, c, h):
+        arrived(other.at[p, some(h, c)], other_recv.at[p, c, h])
+
+    def own_arrived(step, h):
         p = (mine + step) % RING
-        arrived(own.at[p], own_recv.at[p])
-
-    down().start()
-    along(1).start()
-    along(3).start()
+        arrived(own.at[p, some(h)], own_recv.at[p, h])
+
+    for h in range(2):
+        half = slice(h * piece, (h + 1) * piece)
+
+        def layer(i, carry, half=half):
+            at = pl.ds(pl.multiple_of(i * hidden_part, hidden_part), hidden_part)
+            v = jnp.dot(pooled_16[half], w_in_ref[:, at], preferred_element_type=f32)
+            hidden = (v / (1.0 + jnp.exp(-v))).astype(bf16)
+            pooled_sum[half] += jnp.dot(hidden, w_out_ref[at, :], preferred_element_type=f32)
+            return carry
+
+        lax.fori_loop(0, w_in_ref.shape[1] // hidden_part, layer, 0, unroll=4)
+        widened = pooled_sum[half]
+        norm = lax.rsqrt(jnp.sum(widened * widened, axis=1, keepdims=True) + 1e-06)
+        emb[half] = (widened * norm).astype(bf16)
+        down(h).start()
+        along(1, h).start()
+        along(3, h).start()
     own[mine] = emb[...]
-    other_arrived(cross, core)
-    swap(cross).start()
-    across(1).start()
-    across(3).start()
-    along(2).start()
-    own_arrived(1)
-    own_arrived(3)
-    across(2).start()
-    other_arrived(cross, 1 - core)
+
+    for h in range(2):
+        other_arrived(cross, core, h)
+        swap(cross, h).start()
+        across(1, h).start()
+        across(3, h).start()
+    own_arrived(3, 0)
+    along_on(0).start()
+    own_arrived(1, 0)
+    own_arrived(1, 1)
+    along_on(1).start()
+    own_arrived(3, 1)
+    for h in range(2):
+        other_arrived(cross, 1 - core, h)
 
     scale = scale_ref[0, 0]
     to_log2 = scale * LOG2E
@@ -431,22 +472,32 @@
     def pieces(j, carry):
         @pl.when(j == 1)
         def _():
-            own_arrived(2)
-
-        for when, index in ((1, 1), (2, 2), (4, 3)):
-            @pl.when(j == when)
-            def _(index=index):
-                p = (cross + hop(index)) % RING
-                other_arrived(p, core)
-                swap(p).start()
-
-        for when, index in ((1, 1), (3, 2), (5, 3)):
-            @pl.when(j == when)
-            def _(index=index):
-                other_arrived((cross + hop(index)) % RING, 1 - core)
+            own_arrived(2, 0)
+            own_arrived(2, 1)
+            for step in (1, 3):
+                for h in range(2):
+                    p = (cross + step) % RING
+                    other_arrived(p, core, h)
+                    swap(p, h).start()
+            for h in range(2):
+                across_on(h).start()
+
+        @pl.when(j == 4)
+        def _():
+            for h in range(2):
+                p = (cross + 2) % RING
+                other_arrived(p, core, h)
+                swap(p, h).start()
 
         product(2 * j + 1, score_odd)
         gather_sums(2 * j, score_even)
+
+        for when, step in ((1, 1), (3, 3), (5, 2)):
+            @pl.when(j == when)
+            def _(step=step):
+                for h in range(2):
+                    other_arrived((cross + step) % RING, 1 - core, h)
+
         product(jnp.minimum(2 * j + 2, last), score_even)
         gather_sums(2 * j + 1, score_odd)
 
@@ -503,19 +554,21 @@
     hit = fold(jnp.add, [n[2] for n in notes])
     out_ref[...] = scale * (top - hit) + jnp.log(total)
 
-    for step in range(1, SIDE):
-        near_request(step).wait_send()
-        far_request(step).wait_send()
-    gone = outgoing.at[pl.ds(capacity, (groups - 1) * capacity)]
-    arrived(gone, rows_send)
+    arrived(ask.at[pl.ds(0, groups - 1)], ask_send)
+    arrived(outgoing.at[pl.ds(capacity, (groups - 1) * capacity)], rows_send)
     for step in range(1, RING):
         own_label(step).wait_send()
-        along(step).wait_send()
-        across(step).wait_send()
         send_row_note(step).wait_send()
-    down().wait_send()
+    for h in range(2):
+        down(h).wait_send()
+        along_on(h).wait_send()
+        across_on(h).wait_send()
+        for step in (1, 3):
+            along(step, h).wait_send()
+            across(step, h).wait_send()
     for p in range(RING):
-        swap(p).wait_send()
+        for h in range(2):
+            swap(p, h).wait_send()
         for c in range(CORES):
             other_label(p, c).wait_send()
             send_col_note(p, c).wait_send()
@@ -542,10 +595,9 @@
             pltpu.VMEM(w_out.shape, bf16),
             pltpu.VMEM((TABLE_SLOTS, table.shape[0] // TABLE_PARTS, width), bf16),
             pltpu.VMEM(table.shape, f32),
-            pltpu.VMEM((SIDE, SIDE, 1, lanes), i32),
-            pltpu.VMEM((SIDE, SIDE, 1, lanes), i32),
-            pltpu.VMEM((SIDE, SIDE, 1, lanes), i32),
-            pltpu.SMEM((SIDE, SIDE, 1, lanes), i32),
+            pltpu.VMEM((groups, 1, lanes), i32),
+            pltpu.VMEM((groups, 1, lanes), i32),
+            pltpu.SMEM((groups, 1, lanes), i32),
             pltpu.VMEM((capacity, width), f32),
             pltpu.VMEM((slots, width), bf16),
             pltpu.VMEM((slots, width), bf16),
@@ -572,10 +624,10 @@
             pltpu.VMEM((RING, CORES, 3, 1, rows), f32),
             pltpu.VMEM((RING, 3, 1, rows), f32),
             pltpu.VMEM((RING, CORES, 3, 1, rows), f32),
-            dma((2,)), dma((TABLE_PARTS,)), dma((SIDE,)), dma((SIDE,)), dma((SIDE,)), dma((SIDE,)),
+            dma((2,)), dma((TABLE_PARTS,)), pltpu.SemaphoreType.REGULAR, dma, dma((ROUNDS,)),
             dma, dma, dma((ROUNDS,)),
             dma((RING,)), dma((RING,)), dma((RING, CORES)), dma((RING, CORES)),
-            dma((RING,)), dma((RING,)), dma, dma((RING,)), dma((RING,)), dma((RING, CORES)),
+            dma((RING, 2)), dma((RING, 2)), dma((2,)), dma((RING, 2)), dma((RING, 2)), dma((RING, CORES, 2)),
             dma((RING,)), dma((RING,)), dma((RING, CORES)), dma((RING, CORES)),
         ],
         compiler_params=pltpu.CompilerParams(

time: 105 us -> 99.3 us (0.946)
  the two profiles are of different devices: /device:TPU:33 before, /device:TPU:1 now
where the time goes in v3:
time: 99.3 us; the launch traced here: 99.1 us
  Pallas kernels  97.2 us (98%)
  local copies, waits for them, and re-layouts  1.26 us (1%)
    pallas_call x1, Pallas kernels, tower_losses(): pl.pallas_call(kernel, out_shape=jax.ShapeDtypeStruct((1, rows), f32), in...  97.2 us

profile of v3, /device:TPU:1, one launch (start us, length us, event | category | flops | bytes accessed | tf_op | source)
XLA Modules:
  0.0 99.1 jit_solution(14253908253891759989)
XLA Ops:
  0.7 97.2 %tower_losses.1 = f32[1,512]{1,0:T(1,128)} custom-call(s32[8,512]{1,0:T(8,128)} %bitcast.21, s32[8,512]{1,0:T(8,128)} %bitcast.22, s32[8,512]{1,0:T(8,128)} %bitcast.23, f32[8,512]{1,0:T(8,128)} %bitcast.24, s32[1,512]{1,0:T(1,128)} %bitcast.25, f32[1,1]{1,0:T(1,128)} %bitcast.17.scale_ref, bf16[256,2048]{1,0:T(8,128)(2,1)} %bitcast.19, ...), custom_call_target="tpu_custom_call" | custom-call | flops 4294967296 | bytes 8388608 | tf_op jit(solution)/shard_map/tower_losses/pallas_call | solution.py:588
  97.9 1.3 %copy.12 = f32[1,512]{1,0:T(1,128)} copy(f32[1,512]{1,0:T(1,128)} %tower_losses.1) | data formatting | bytes 4096

commit v4 on v3

--- a/solution.py
+++ b/solution.py
@@ -11,49 +11,17 @@
 SIDE = 8
 TABLE_PARTS = 16
 TABLE_SLOTS = 6
-ROUNDS = 4
+ROUNDS = 8
 TURNS = SIDE * SIDE // ROUNDS
+IN_FLIGHT = 14
 FIRST = 2 * SIDE - 1
 LOG2E = 1.4426950408889634
 LOWEST = -1e30
 MESH = pl.DeviceIdType.MESH
 
 
-def whereabouts():
-    tower = lax.axis_index("tower")
-    shard = lax.axis_index("shard")
-    return tower, shard // 16, shard // 8 % 2, shard // 2 % 4, shard % 2
-
-
-def shard_at(y, x_hi, z, core):
-    return ((y * 2 + x_hi) * 4 + z) * 2 + core
-
-
-def own_line(position, core=None):
-    tower, y, x_hi, z, c = whereabouts()
-    c = c if core is None else core
-    return shard_at(y + tower * (position - y), x_hi, z + (1 - tower) * (position - z), c)
-
-
-def cross_line(position):
-    tower, y, x_hi, z, c = whereabouts()
-    return shard_at(y + (1 - tower) * (position - y), x_hi, z + tower * (position - z), c)
-
-
-def below_line(position, core):
-    tower, y, x_hi, z, _ = whereabouts()
-    plane = x_hi * tower + (1 - x_hi) * (1 - tower)
-    return shard_at(y + tower * (position - y), plane, z + (1 - tower) * (position - z), core)
-
-
-def above_line(position, core):
-    tower, y, x_hi, z, _ = whereabouts()
-    plane = x_hi * (1 - tower) + (1 - x_hi) * tower
-    return shard_at(y + (1 - tower) * (position - y), plane, z + tower * (position - z), core)
-
-
-def hop(i):
-    return i + i // 2 - 2 * (i // 3)
+def wrapped(i, size):
+    return jnp.where(i >= size, i - size, i)
 
 
 def fold(op, parts):
@@ -99,11 +67,30 @@
     bag, rows = owner_ref.shape
     groups, lanes = SIDE * SIDE, ask.shape[2]
     capacity = outgoing.shape[0] // groups
-    tower, y, x_hi, z, core = whereabouts()
-    me = lax.axis_index("shard")
+    tower, me = lax.axis_index("tower"), lax.axis_index("shard")
     far, near = me // SIDE, me % SIDE
+    y, x_hi, z, core = far // 2, far % 2, near // CORES, near % CORES
     mine = z + tower * (y - z)
     cross = y + tower * (z - y)
+    mine_at = [wrapped(mine + i, RING) for i in range(RING)]
+    cross_at = [wrapped(cross + i, RING) for i in range(RING)]
+
+    def shard_at(y, x_hi, z, core):
+        return ((y * 2 + x_hi) * RING + z) * CORES + core
+
+    def own_line(position, core=core):
+        return shard_at(y + tower * (position - y), x_hi, z + (1 - tower) * (position - z), core)
+
+    def cross_line(position):
+        return shard_at(y + (1 - tower) * (position - y), x_hi, z + tower * (position - z), core)
+
+    def below_line(position, core):
+        plane = x_hi * tower + (1 - x_hi) * (1 - tower)
+        return shard_at(y + tower * (position - y), plane, z + (1 - tower) * (position - z), core)
+
+    def above_line(position, core):
+        plane = x_hi * (1 - tower) + (1 - x_hi) * tower
+        return shard_at(y + (1 - tower) * (position - y), plane, z + tower * (position - z), core)
 
     part = table_16.shape[1]
     loads = []
@@ -119,12 +106,15 @@
 
     barrier = pltpu.get_barrier_semaphore()
 
+    def neighbour(step_far, step_near):
+        return wrapped(far + step_far, SIDE) * SIDE + wrapped(near + step_near, SIDE)
+
     def greet(tower_id, shard_id):
         pl.semaphore_signal(barrier, inc=1, device_id=(tower_id, shard_id), device_id_type=MESH)
 
     for step in range(1, SIDE):
-        greet(tower, far * SIDE + (near + step) % SIDE)
-        greet(tower, (far + step) % SIDE * SIDE + near)
+        greet(tower, neighbour(0, step))
+        greet(tower, neighbour(step, 0))
     greet(1 - tower, below_line(mine, core))
     greet(1 - tower, above_line(cross, core))
 
@@ -159,27 +149,6 @@
     for g in range(groups):
         ask[g] = wanted[g : g + 1]
 
-    pl.semaphore_wait(barrier, 2 * SIDE)
-
-    for step in range(1, SIDE):
-        pl.semaphore_signal(known, inc=1, device_id=(tower, (far + step) % SIDE * SIDE + near),
-                            device_id_type=MESH)
-
-    def neighbour(step_far, step_near):
-        return (far + step_far) % SIDE * SIDE + (near + step_near) % SIDE
-
-    def later_steps(i):
-        later = i - FIRST
-        return 1 + later % (SIDE - 1), 1 + (later + later // (SIDE - 1)) % (SIDE - 1)
-
-    def request(i, to):
-        return remote(ask.at[to], asked.at[i], ask_send, ask_recv.at[i // TURNS], tower, to)
-
-    for i in range(1, SIDE):
-        request(i, neighbour(0, i)).start()
-    for i in range(1, SIDE):
-        request(SIDE - 1 + i, neighbour(i, 0)).start()
-    asked[0] = ask[me]
     def widen(i):
         loads[i].wait()
 
@@ -193,89 +162,48 @@
         if i + TABLE_SLOTS < TABLE_PARTS:
             loads[i + TABLE_SLOTS].start()
 
-    def send_requests(first, end):
-        def send(i, carry):
-            request(i, neighbour(*later_steps(i))).start()
-            return carry
-
-        lax.fori_loop(first, end, send, 0)
-
-    for i in range(TABLE_PARTS // 2):
-        widen(i)
-    pl.semaphore_wait(known, SIDE - 1)
-    send_requests(FIRST, TURNS)
-    for i in range(TABLE_PARTS // 2, TABLE_PARTS):
+    for i in range(TABLE_PARTS):
         widen(i)
     for load in weight_loads:
         load.start()
 
-    def block_of(ref, i):
-        return ref.at[pl.ds(pl.multiple_of(i * capacity, 16), capacity)]
-
-    def look_up(i, destination):
-        for c in range(capacity):
-            row = jnp.clip(asked_at[i, 0, c], 0, table_32.shape[0] - 1)
-            staged[c : c + 1] = table_32[pl.ds(row, 1)]
-        destination[...] = staged[...].astype(bf16)
-
-    def serve(i, to):
-        block = block_of(outgoing, i)
-        look_up(i, block)
-        remote(block, block_of(fetched, i), rows_send, rows_recv.at[i // TURNS], tower, to).start()
-
-    def serve_near(i, carry):
-        serve(i, neighbour(0, SIDE - i))
-        return carry
-
-    def serve_far(i, carry):
-        serve(i, neighbour(FIRST - i, 0))
-        return carry
-
-    def serve_later(i, carry):
-        step_far, step_near = later_steps(i)
-        serve(i, neighbour(SIDE - step_far, SIDE - step_near))
-        return carry
-
-    for n in range(ROUNDS):
-        first, end = max(n * TURNS, 1), (n + 1) * TURNS
-        arrived(asked.at[pl.ds(first, end - first)], ask_recv.at[n])
-        to_scalar = pltpu.make_async_copy(
-            asked.at[pl.ds(n * TURNS, TURNS)], asked_at.at[pl.ds(n * TURNS, TURNS)], asked_sem)
-        to_scalar.start()
-        if n + 1 < ROUNDS:
-            send_requests(end, end + TURNS)
-        to_scalar.wait()
-        if n == 0:
-            lax.fori_loop(SIDE, FIRST, serve_far, 0)
-            lax.fori_loop(1, SIDE, serve_near, 0)
-            first = FIRST
-        lax.fori_loop(first, end, serve_later, 0)
-    look_up(0, block_of(fetched, 0))
-
-    def own_label(step):
-        return remote(labels_ref, own_labels.at[mine], own_label_send.at[step], own_label_recv.at[mine],
-                      tower, own_line((mine + step) % RING))
-
-    def other_label(p, c):
-        return remote(labels_ref, other_labels.at[z, core], other_label_send.at[p, c],
-                      other_label_recv.at[z, core], tower, shard_at(y, 1 - x_hi, p, c))
-
-    for step in range(1, RING):
-        own_label(step).start()
-    for p in range(RING):
-        for c in range(CORES):
-            other_label(p, c).start()
-    own_labels[mine] = labels_ref[...]
+    pl.semaphore_wait(barrier, 2 * SIDE)
+
+    for step in range(1, SIDE):
+        pl.semaphore_signal(known, inc=1, device_id=(tower, neighbour(step, 0)),
+                            device_id_type=MESH)
+
+    def request(i, to, later):
+        return remote(ask.at[to], asked.at[i], ask_send, ask_recv.at[later], tower, to)
+
+    for i in range(1, SIDE):
+        request(SIDE - 1 + i, neighbour(i, 0), 0).start()
+        request(i, neighbour(0, i), 0).start()
+    pl.semaphore_wait(known, SIDE - 1)
+    short = SIDE - 1
+
+    def later_turns(do):
+        def outer(q, carry):
+            def inner(r, carry):
+                do(FIRST + short * q + r, 1 + r, 1 + wrapped(q + r, short))
+                return carry
+
+            return lax.fori_loop(0, short, inner, carry)
+
+        lax.fori_loop(0, short, outer, 0)
+
+    later_turns(lambda i, step_far, step_near: request(i, neighbour(step_far, step_near), 1).start())
 
     target_wide, weight_wide = score_even, score_odd
     for k in range(bag):
-        target_wide[:, k * lanes : (k + 1) * lanes] = jnp.transpose(
+        at = slice(k * lanes, (k + 1) * lanes)
+        target_wide[:, at] = jnp.transpose(
             jnp.broadcast_to(first_slot[k : k + 1, :] + slots[k], (lanes, rows)))
-        weight_wide[:, k * lanes : (k + 1) * lanes] = jnp.transpose(jnp.broadcast_to(weight_ref[k : k + 1, :], (lanes, rows)))
+        weight_wide[:, at] = jnp.transpose(jnp.broadcast_to(weight_ref[k : k + 1, :], (lanes, rows)))
     lane = lax.broadcasted_iota(jnp.int32, (16, lanes), 1).astype(f32)
     spread = mix_high.shape[1] // lanes
 
-    def weigh(i, carry):
+    def weigh(i):
         at = pl.ds(pl.multiple_of(i * 16, 16), 16)
         targets = [target_wide[at, k * lanes : (k + 1) * lanes] for k in range(bag)]
         weights = [weight_wide[at, k * lanes : (k + 1) * lanes] for k in range(bag)]
@@ -291,12 +219,69 @@
             mix_low[at, cols] = (mixed - high.astype(f32)).astype(bf16)
             return carry
 
-        return lax.fori_loop(0, spread, column, carry, unroll=4)
-
-    lax.fori_loop(0, rows // 16, weigh, 0)
+        lax.fori_loop(0, spread, column, 0, unroll=4)
+
+    def block_of(ref, i):
+        return ref.at[pl.ds(pl.multiple_of(i * capacity, 16), capacity)]
+
+    def look_up(i, destination):
+        for c in range(capacity):
+            row = jnp.clip(asked_at[i, 0, c], 0, table_32.shape[0] - 1)
+            staged[c : c + 1] = table_32[pl.ds(row, 1)]
+        destination[...] = staged[...].astype(bf16)
+
+    def rows_to(i, to, round_of):
+        return remote(block_of(outgoing, i), block_of(fetched, i), rows_send.at[i], rows_recv.at[round_of],
+                      tower, to)
+
+    def serve(i, to, round_of):
+        look_up(i, block_of(outgoing, i))
+        rows_to(i, to, round_of).start()
+
+    def rows_gone(i):
+        arrived(block_of(outgoing, i), rows_send.at[i])
+
+    def serve_later(i, step_far, step_near):
+        rows_gone(i - IN_FLIGHT)
+        serve(i, neighbour(SIDE - step_far, SIDE - step_near), i // TURNS)
+
+        @pl.when(i - FIRST < rows // 16)
+        def _():
+            weigh(i - FIRST)
+
+    def own_label(step):
+        return remote(labels_ref, own_labels.at[mine], own_label_send.at[step], own_label_recv.at[mine],
+                      tower, own_line(mine_at[step]))
+
+    def other_label(p, c):
+        return remote(labels_ref, other_labels.at[z, core], other_label_send.at[p, c],
+                      other_label_recv.at[z, core], tower, shard_at(y, 1 - x_hi, p, c))
+
+    for n, (first, end) in enumerate(((1, FIRST), (FIRST, groups))):
+        arrived(asked.at[pl.ds(first, end - first)], ask_recv.at[n])
+        here = pl.ds(first, end - first)
+        to_scalar = pltpu.make_async_copy(asked.at[here], asked_at.at[here], asked_sem)
+        to_scalar.start()
+        to_scalar.wait()
+        if n == 0:
+            for i in range(1, SIDE):
+                serve(short + i, neighbour(SIDE - i, 0), (short + i) // TURNS)
+                serve(i, neighbour(0, SIDE - i), i // TURNS)
+        else:
+            for step in range(1, RING):
+                own_label(step).start()
+            for p in range(RING):
+                for c in range(CORES):
+                    other_label(p, c).start()
+            own_labels[mine] = labels_ref[...]
+            later_turns(serve_later)
+    to_scalar = pltpu.make_async_copy(ask.at[me], asked_at.at[0], asked_sem)
+    to_scalar.start()
+    to_scalar.wait()
+    look_up(0, block_of(fetched, 0))
 
     for step in range(1, RING):
-        p = (mine + step) % RING
+        p = mine_at[step]
         arrived(own_labels.at[p], own_label_recv.at[p])
     for p in range(RING):
         for c in range(CORES):
@@ -316,10 +301,10 @@
     deep = TURNS * capacity
     pooled_sum[...] = jnp.zeros(pooled_sum.shape, f32)
     for i in range(ROUNDS):
-        first = capacity if i == 0 else i * deep
-        landed = fetched.at[pl.ds(first, (i + 1) * deep - first)]
-        arrived(landed, rows_recv.at[i])
-        at = slice(i * deep, (i + 1) * deep)
+        start, end = i * deep, (i + 1) * deep
+        first = max(start, capacity)
+        arrived(fetched.at[pl.ds(first, end - first)], rows_recv.at[i])
+        at = slice(start, end)
         data = fetched[at]
         pooled_sum[...] += (
             jnp.dot(mix_high[:, at], data, preferred_element_type=f32)
@@ -340,24 +325,24 @@
 
     def along(step, h):
         return remote(emb.at[some(h)], own.at[mine, some(h)], own_send.at[step, h], own_recv.at[mine, h],
-                      tower, own_line((mine + step) % RING))
+                      tower, own_line(mine_at[step]))
 
     def along_on(h):
-        p = (mine + 3 - 2 * h) % RING
+        p = mine_at[3 - 2 * h]
         here = own.at[p, some(h)]
         return remote(here, here, own_send.at[2, h], own_recv.at[p, h],
-                      tower, own_line((mine + 1 + 2 * h) % RING))
+                      tower, own_line(mine_at[1 + 2 * h]))
 
     def across(step, h):
         here = other.at[cross, some(h, core)]
         return remote(here, here, cross_send.at[step, h], other_recv.at[cross, core, h],
-                      tower, cross_line((cross + step) % RING))
+                      tower, cross_line(cross_at[step]))
 
     def across_on(h):
-        p = (cross + 3 - 2 * h) % RING
+        p = cross_at[3 - 2 * h]
         here = other.at[p, some(h, core)]
         return remote(here, here, cross_send.at[2, h], other_recv.at[p, core, h],
-                      tower, cross_line((cross + 1 + 2 * h) % RING))
+                      tower, cross_line(cross_at[1 + 2 * h]))
 
     def swap(p, h):
         here = other.at[p, some(h, core)]
@@ -368,7 +353,7 @@
         arrived(other.at[p, some(h, c)], other_recv.at[p, c, h])
 
     def own_arrived(step, h):
-        p = (mine + step) % RING
+        p = mine_at[step]
         arrived(own.at[p, some(h)], own_recv.at[p, h])
 
     for h in range(2):
@@ -377,7 +362,8 @@
         def layer(i, carry, half=half):
             at = pl.ds(pl.multiple_of(i * hidden_part, hidden_part), hidden_part)
             v = jnp.dot(pooled_16[half], w_in_ref[:, at], preferred_element_type=f32)
-            hidden = (v / (1.0 + jnp.exp(-v))).astype(bf16)
+            v = 0.5 * v
+            hidden = (v + v * jnp.tanh(v)).astype(bf16)
             pooled_sum[half] += jnp.dot(hidden, w_out_ref[at, :], preferred_element_type=f32)
             return carry
 
@@ -408,15 +394,11 @@
     to_log2 = scale * LOG2E
     strip = 16
 
-    def product(step, destination):
-        p = (cross + hop(step // RING)) % RING
-        a = (mine + hop(step % RING)) % RING
+    def product(p, a, destination):
         destination[...] = lax.dot_general(own[a], other[p], (((1,), (1,)), ((), ())),
                                            preferred_element_type=f32)
 
-    def gather_sums(step, source):
-        p = (cross + hop(step // RING)) % RING
-        a = (mine + hop(step % RING)) % RING
+    def gather_sums(p, a, source):
         col_old = col_max[p]
 
         def tops(r, carry):
@@ -466,17 +448,26 @@
         return remote(col_note.at[p, c], col_post.at[cross, core], col_send.at[p, c], col_recv.at[cross, core],
                       1 - tower, above_line(p, c))
 
-    last = RING * RING - 1
-    product(0, score_even)
+    product(cross, mine, score_even)
+
+    def at_least(j, n):
+        return jnp.where(j >= n, 1, 0)
 
     def pieces(j, carry):
+        g = at_least(j, 2) + at_least(j, 4) + at_least(j, 6)
+        late = j - 2 * g
+        upcoming = jnp.minimum(g + late, RING - 1)
+        p = wrapped(cross + g + at_least(g, 2) - 2 * at_least(g, 3), RING)
+        p_next = wrapped(cross + upcoming + at_least(upcoming, 2) - 2 * at_least(upcoming, 3), RING)
+        first, second, third = [wrapped(mine + i, RING) for i in (3 * late, 1 + late, 3 - 3 * late)]
+
         @pl.when(j == 1)
         def _():
             own_arrived(2, 0)
             own_arrived(2, 1)
             for step in (1, 3):
                 for h in range(2):
-                    p = (cross + step) % RING
+                    p = cross_at[step]
                     other_arrived(p, core, h)
                     swap(p, h).start()
             for h in range(2):
@@ -485,25 +476,24 @@
         @pl.when(j == 4)
         def _():
             for h in range(2):
-                p = (cross + 2) % RING
+                p = cross_at[2]
                 other_arrived(p, core, h)
                 swap(p, h).start()
 
-        product(2 * j + 1, score_odd)
-        gather_sums(2 * j, score_even)
+        product(p, second, score_odd)
+        gather_sums(p, first, score_even)
 
         for when, step in ((1, 1), (3, 3), (5, 2)):
             @pl.when(j == when)
             def _(step=step):
                 for h in range(2):
-                    other_arrived((cross + step) % RING, 1 - core, h)
-
-        product(jnp.minimum(2 * j + 2, last), score_even)
-        gather_sums(2 * j + 1, score_odd)
-
-        @pl.when(j % 2 == 1)
+                    other_arrived(cross_at[step], 1 - core, h)
+
+        product(p_next, third, score_even)
+        gather_sums(p, second, score_odd)
+
+        @pl.when(late == 1)
         def _():
-            p = (cross + hop(j // 2)) % RING
             top = jnp.max(col_max[p], axis=0, keepdims=True)
             total = jnp.sum(col_sum[p] * jnp.exp2((col_max[p] - top) * to_log2), axis=0, keepdims=True)
             hit = jnp.sum(col_hit[p], axis=0, keepdims=True)
@@ -519,7 +509,7 @@
     wide_lane = lax.broadcasted_iota(jnp.int32, (rows, 128), 1)
 
     def send_row_note(step):
-        p = (mine + step) % RING
+        p = mine_at[step]
         return remote(row_note.at[p], row_post.at[mine], row_send.at[step], row_recv.at[mine],
                       tower, own_line(p))
 
@@ -532,13 +522,9 @@
         for n in range(3):
             row_note[a, n] = packed[n : n + 1]
 
-    def row_results(i, carry):
-        step = i + 1
-        row_totals((mine + step) % RING)
+    for step in (1, 2, 3):
+        row_totals(mine_at[step])
         send_row_note(step).start()
-        return carry
-
-    lax.fori_loop(0, RING - 1, row_results, 0)
     row_totals(mine)
     notes = [[row_note[mine, n] for n in range(3)]]
     for p in range(RING):
@@ -546,7 +532,7 @@
             arrived(col_post.at[p, c], col_recv.at[p, c])
             notes.append([col_post[p, c, n] for n in range(3)])
     for step in (1, 2, 3):
-        p = (mine + step) % RING
+        p = mine_at[step]
         arrived(row_post.at[p], row_recv.at[p])
         notes.append([row_post[p, n] for n in range(3)])
     top = fold(jnp.maximum, [n[0] for n in notes])
@@ -555,7 +541,12 @@
     out_ref[...] = scale * (top - hit) + jnp.log(total)
 
     arrived(ask.at[pl.ds(0, groups - 1)], ask_send)
-    arrived(outgoing.at[pl.ds(capacity, (groups - 1) * capacity)], rows_send)
+
+    def last_rows_gone(i, carry):
+        rows_gone(i)
+        return carry
+
+    lax.fori_loop(groups - IN_FLIGHT, groups, last_rows_gone, 0)
     for step in range(1, RING):
         own_label(step).wait_send()
         send_row_note(step).wait_send()
@@ -624,8 +615,8 @@
             pltpu.VMEM((RING, CORES, 3, 1, rows), f32),
             pltpu.VMEM((RING, 3, 1, rows), f32),
             pltpu.VMEM((RING, CORES, 3, 1, rows), f32),
-            dma((2,)), dma((TABLE_PARTS,)), pltpu.SemaphoreType.REGULAR, dma, dma((ROUNDS,)),
-            dma, dma, dma((ROUNDS,)),
+            dma((2,)), dma((TABLE_PARTS,)), pltpu.SemaphoreType.REGULAR, dma, dma((2,)),
+            dma, dma((groups,)), dma((ROUNDS,)),
             dma((RING,)), dma((RING,)), dma((RING, CORES)), dma((RING, CORES)),
             dma((RING, 2)), dma((RING, 2)), dma((2,)), dma((RING, 2)), dma((RING, 2)), dma((RING, CORES, 2)),
             dma((RING,)), dma((RING,)), dma((RING, CORES)), dma((RING, CORES)),

time: 99.3 us -> 90.9 us (0.915)
  Pallas kernels: 97.2 us -> 88.8 us
    pallas_call x1, Pallas kernels: 97.2 us -> 88.8 us  [tower_losses(): pl.pallas_call(kernel, out_shape=jax.ShapeDtypeStruct((1, rows), f32), in...]
where the time goes in v4:
time: 90.9 us; the launch traced here: 90.7 us
  Pallas kernels  88.8 us (98%)
  local copies, waits for them, and re-layouts  1.26 us (1%)
    pallas_call x1, Pallas kernels, tower_losses(): pl.pallas_call(kernel, out_shape=jax.ShapeDtypeStruct((1, rows), f32), in...  88.8 us

profile of v4, /device:TPU:1, one launch (start us, length us, event | category | flops | bytes accessed | tf_op | source)
XLA Modules:
  0.0 90.7 jit_solution(6104525615562377329)
XLA Ops:
  0.7 88.8 %tower_losses.1 = f32[1,512]{1,0:T(1,128)} custom-call(s32[8,512]{1,0:T(8,128)} %bitcast.21, s32[8,512]{1,0:T(8,128)} %bitcast.22, s32[8,512]{1,0:T(8,128)} %bitcast.23, f32[8,512]{1,0:T(8,128)} %bitcast.24, s32[1,512]{1,0:T(1,128)} %bitcast.25, f32[1,1]{1,0:T(1,128)} %bitcast.17.scale_ref, bf16[256,2048]{1,0:T(8,128)(2,1)} %bitcast.19, ...), custom_call_target="tpu_custom_call" | custom-call | flops 4294967296 | bytes 8388608 | tf_op jit(solution)/shard_map/tower_losses/pallas_call | solution.py:579
  89.4 1.3 %copy.12 = f32[1,512]{1,0:T(1,128)} copy(f32[1,512]{1,0:T(1,128)} %tower_losses.1) | data formatting | bytes 4096

commit v5 on v4

--- a/solution.py
+++ b/solution.py
@@ -403,14 +403,16 @@
 
         def tops(r, carry):
             at = pl.ds(r * strip, strip)
-            s = source[at]
+            s = source[at].astype(bf16)
             old = row_max[a, at]
-            new = jnp.maximum(old, fold(jnp.maximum, lane_groups(s)))
+            new = jnp.maximum(old, fold(jnp.maximum, lane_groups(s)).astype(f32))
             row_sum[a, at] = row_sum[a, at] * jnp.exp2((old - new) * to_log2)
             row_max[a, at] = new
-            return jnp.maximum(carry, fold(jnp.maximum, sublane_groups(s)))
-
-        col_new = lax.fori_loop(0, rows // strip, tops, col_old, unroll=True)
+            return jnp.maximum(carry, s)
+
+        tallest = jnp.full((strip, CORES * rows), LOWEST, bf16)
+        tallest = lax.fori_loop(0, rows // strip, tops, tallest, unroll=True).astype(f32)
+        col_new = jnp.maximum(col_old, fold(jnp.maximum, sublane_groups(tallest)))
         col_max[p] = col_new
         col_top = col_new * to_log2
         key = col_key[p]
@@ -538,7 +540,8 @@
     top = fold(jnp.maximum, [n[0] for n in notes])
     total = fold(jnp.add, [n[1] * jnp.exp2((n[0] - top) * to_log2) for n in notes])
     hit = fold(jnp.add, [n[2] for n in notes])
-    out_ref[...] = scale * (top - hit) + jnp.log(total)
+    out_ref[0:1, :] = scale * (top - hit)
+    out_ref[1:2, :] = total
 
     arrived(ask.at[pl.ds(0, groups - 1)], ask_send)
 
@@ -578,7 +581,7 @@
     anywhere = pl.BlockSpec(memory_space=pl.ANY)
     return pl.pallas_call(
         kernel,
-        out_shape=jax.ShapeDtypeStruct((1, rows), f32),
+        out_shape=jax.ShapeDtypeStruct((2, rows), f32),
         in_specs=[vmem] * 5 + [pl.BlockSpec(memory_space=pltpu.SMEM)] + [anywhere] * 3,
         out_specs=vmem,
         scratch_shapes=[
@@ -634,10 +637,11 @@
 def per_device(
     tables, bag_owner, bag_block, bag_offset, bag_weight, w_in, w_out, labels, logit_scale
 ):
-    return tower_losses(
+    parts = tower_losses(
         tables[0], bag_owner[0].T, bag_block[0].T, bag_offset[0].T, bag_weight[0].T, w_in[0], w_out[0],
         labels, logit_scale,
     )
+    return parts[0:1] + jnp.log(parts[1:2])
 
 
 def solution(mesh):

time: 90.9 us -> 90.5 us (level)
  other arithmetic: 0 us -> 1.35 us
  local copies, waits for them, and re-layouts: 1.26 us -> 0 us
    add x0 -> x1, other arithmetic: none -> 1.35 us  [per_device(): return parts[0:1] + jnp.log(parts[1:2])]
    unnamed x1 -> x0, local copies, waits for them, and re-layouts: 1.26 us -> none
where the time goes in v5:
time: 90.5 us; the launch traced here: 90.3 us
  Pallas kernels  88.3 us (98%)
  other arithmetic  1.35 us (1%)
    pallas_call x1, Pallas kernels, tower_losses(): pl.pallas_call(kernel, out_shape=jax.ShapeDtypeStruct((2, rows), f32), in...  88.3 us

profile of v5, /device:TPU:1, one launch (start us, length us, event | category | flops | bytes accessed | tf_op | source)
XLA Modules:
  0.0 90.3 jit_solution(10273903688339000975)
XLA Ops:
  0.7 88.3 %tower_losses.1 = f32[2,512]{1,0:T(2,128)} custom-call(s32[8,512]{1,0:T(8,128)} %bitcast.21, s32[8,512]{1,0:T(8,128)} %bitcast.22, s32[8,512]{1,0:T(8,128)} %bitcast.23, f32[8,512]{1,0:T(8,128)} %bitcast.24, s32[1,512]{1,0:T(1,128)} %bitcast.25, f32[1,1]{1,0:T(1,128)} %bitcast.17.scale_ref, bf16[256,2048]{1,0:T(8,128)(2,1)} %bitcast.19, ...), custom_call_target="tpu_custom_call" | custom-call | flops 4294967296 | bytes 8388608 | tf_op jit(solution)/shard_map/tower_losses/pallas_call | solution.py:582
  88.9 1.3 %log_add_fusion = f32[1,512]{1,0:T(1,128)} fusion(f32[2,512]{1,0:T(2,128)} %tower_losses.1), kind=kLoop, calls=%fused_computation | loop fusion | flops 512 | bytes 6144 | tf_op jit(solution)/shard_map/add | solution.py:644

commit v6 on v5

--- a/solution.py
+++ b/solution.py
@@ -528,6 +528,28 @@
         row_totals(mine_at[step])
         send_row_note(step).start()
     row_totals(mine)
+    arrived(ask.at[pl.ds(0, groups - 1)], ask_send)
+
+    def last_rows_gone(i, carry):
+        rows_gone(i)
+        return carry
+
+    lax.fori_loop(groups - IN_FLIGHT, groups, last_rows_gone, 0)
+    for step in range(1, RING):
+        own_label(step).wait_send()
+    for h in range(2):
+        down(h).wait_send()
+        along_on(h).wait_send()
+        across_on(h).wait_send()
+        for step in (1, 3):
+            along(step, h).wait_send()
+            across(step, h).wait_send()
+    for p in range(RING):
+        for h in range(2):
+            swap(p, h).wait_send()
+        for c in range(CORES):
+            other_label(p, c).wait_send()
+
     notes = [[row_note[mine, n] for n in range(3)]]
     for p in range(RING):
         for c in range(CORES):
@@ -542,29 +564,10 @@
     hit = fold(jnp.add, [n[2] for n in notes])
     out_ref[0:1, :] = scale * (top - hit)
     out_ref[1:2, :] = total
-
-    arrived(ask.at[pl.ds(0, groups - 1)], ask_send)
-
-    def last_rows_gone(i, carry):
-        rows_gone(i)
-        return carry
-
-    lax.fori_loop(groups - IN_FLIGHT, groups, last_rows_gone, 0)
     for step in range(1, RING):
-        own_label(step).wait_send()
         send_row_note(step).wait_send()
-    for h in range(2):
-        down(h).wait_send()
-        along_on(h).wait_send()
-        across_on(h).wait_send()
-        for step in (1, 3):
-            along(step, h).wait_send()
-            across(step, h).wait_send()
     for p in range(RING):
-        for h in range(2):
-            swap(p, h).wait_send()
         for c in range(CORES):
-            other_label(p, c).wait_send()
             send_col_note(p, c).wait_send()
 
 

time: 90.5 us -> 90.4 us (level)
  no operation moved by 1% of the time
where the time goes in v6:
time: 90.4 us; the launch traced here: 90.1 us
  Pallas kernels  88.1 us (97%)
  other arithmetic  1.35 us (1%)
    pallas_call x1, Pallas kernels, tower_losses(): pl.pallas_call(kernel, out_shape=jax.ShapeDtypeStruct((2, rows), f32), in...  88.1 us

profile of v6, /device:TPU:1, one launch (start us, length us, event | category | flops | bytes accessed | tf_op | source)
XLA Modules:
  0.0 90.1 jit_solution(13645608868669915360)
XLA Ops:
  0.7 88.1 %tower_losses.1 = f32[2,512]{1,0:T(2,128)} custom-call(s32[8,512]{1,0:T(8,128)} %bitcast.21, s32[8,512]{1,0:T(8,128)} %bitcast.22, s32[8,512]{1,0:T(8,128)} %bitcast.23, f32[8,512]{1,0:T(8,128)} %bitcast.24, s32[1,512]{1,0:T(1,128)} %bitcast.25, f32[1,1]{1,0:T(1,128)} %bitcast.17.scale_ref, bf16[256,2048]{1,0:T(8,128)(2,1)} %bitcast.19, ...), custom_call_target="tpu_custom_call" | custom-call | flops 4294967296 | bytes 8388608 | tf_op jit(solution)/shard_map/tower_losses/pallas_call | solution.py:585
  88.8 1.3 %log_add_fusion = f32[1,512]{1,0:T(1,128)} fusion(f32[2,512]{1,0:T(2,128)} %tower_losses.1), kind=kLoop, calls=%fused_computation | loop fusion | flops 512 | bytes 6144 | tf_op jit(solution)/shard_map/add | solution.py:647
